TPU v7x, 128 devices: a whole 4x4x4 slice. The times are simulated.
128 devices in a mesh: row: 8 (over y_hi, z), col: 16 (over y_lo, x, core).
Axes of the slice: x: 4, y: 4 (y_hi: 2, y_lo: 2; y = y_hi * 2 + y_lo), z: 4, core: 2. Of those that a mesh axis runs over, the one named last changes fastest.
Arguments:
- frames: bfloat16 [16, 256, 256, 128], P(None, 'row', 'col'), may hold values from -6 to 6
- cotangent: bfloat16 [16, 256, 256, 128], P(None, 'row', 'col'), may hold values from -6 to 6
- first_norm_gain: float32 [128], replicated, may hold values from 0.1 to 1.9
- w_qkv: bfloat16 [128, 384], replicated, may hold values from -0.5 to 0.5
- rel_bias: float32 [4, 256, 256], replicated, may hold values from -4 to 4
- w_proj: bfloat16 [128, 128], replicated, may hold values from -0.5 to 0.5
- second_norm_gain: float32 [128], replicated, may hold values from 0.1 to 1.9
- w_up: bfloat16 [128, 512], replicated, may hold values from -0.5 to 0.5
- w_down: bfloat16 [512, 128], replicated, may hold values from -0.25 to 0.25
Outputs:
- frames_input_gradient: float32 [16, 256, 256, 128], P(None, 'row', 'col')
- g_qkv: float32 [128, 384], replicated
- g_proj: float32 [128, 128], replicated
- g_up: float32 [128, 512], replicated
- g_down: float32 [512, 128], replicated
All inputs are finite; a program needn't handle non-finite values.
Results may differ from a plain program's by a relative error of at most 0.015.
Values may be sent and summed in bfloat16 or wider, within the bound.
A program may use at most 192 MiB of HBM per device.

v0:
```python
import math

import jax
import jax.numpy as jnp
from jax import lax
from jax.sharding import PartitionSpec as P

HEADS = 4
WS = 16
SHIFT = 8


EPS = 1e-05


def from_behind(block, axis, distance):
    devices = range(lax.axis_size(axis))
    route = [((i - distance) % len(devices), i) for i in devices]
    return lax.ppermute(block, axis, route)


def layer_norm_forward(x, norm_gain_vector):
    xf = x.astype(jnp.float32)
    centered_values = xf - jnp.mean(xf, -1, keepdims=True)
    inverse_deviation = lax.rsqrt(
        jnp.mean(centered_values * centered_values, -1, keepdims=True) + EPS
    )
    normalized_input = centered_values * inverse_deviation
    return (normalized_input * norm_gain_vector, normalized_input, inverse_deviation)


def layer_norm_backward(upstream_gradient, norm_gain_vector, normalized_input, inverse_deviation):
    normalized_gradient = upstream_gradient * norm_gain_vector
    return inverse_deviation * (
        normalized_gradient
        - jnp.mean(normalized_gradient, -1, keepdims=True)
        - normalized_input * jnp.mean(normalized_gradient * normalized_input, -1, keepdims=True)
    )


def split_windows(t, ws):
    f, h, w, c = t.shape
    t = t.reshape(f, h // ws, ws, w // ws, ws, c).transpose(0, 1, 3, 2, 4, 5)
    return t.reshape(f * (h // ws) * (w // ws), ws * ws, c)


def merge_windows(t, f, h, w, ws):
    c = t.shape[-1]
    t = t.reshape(f, h // ws, w // ws, ws, ws, c).transpose(0, 1, 3, 2, 4, 5)
    return t.reshape(f, h, w, c)


def regions(start, count, total, ws, sh):
    pos = start + jnp.arange(count, dtype=jnp.int32)
    return jnp.where(pos < total - ws, 0, jnp.where(pos < total - sh, 1, 2)).astype(jnp.int32)


def gelu_parts(u):
    cdf = 0.5 * (1.0 + jax.scipy.special.erf(u * (1.0 / math.sqrt(2.0))))
    dens = jnp.exp(-0.5 * u * u) * (1.0 / math.sqrt(2.0 * math.pi))
    return (u * cdf, cdf + u * dens)


def roll_ahead(tile, sh):
    right = from_behind(tile[:, :, :sh], "col", -1)
    wide = jnp.concatenate([tile[:, :, sh:], right], 2)
    lower = from_behind(wide[:, :sh], "row", -1)
    return jnp.concatenate([wide[:, sh:], lower], 1)


def roll_behind(tile, sh):
    left = from_behind(tile[:, :, -sh:], "col", 1)
    wide = jnp.concatenate([left, tile[:, :, :-sh]], 2)
    upper = from_behind(wide[:, -sh:], "row", 1)
    return jnp.concatenate([upper, wide[:, :-sh]], 1)


def probabilities(qkv, labels, rel_bias, heads):
    b, l, c3 = qkv.shape
    c = c3 // 3
    hd = c // heads
    query = qkv[..., :c].reshape(b, l, heads, hd)
    keys = qkv[..., c : 2 * c].reshape(b, l, heads, hd)
    values = qkv[..., 2 * c :].reshape(b, l, heads, hd)
    scores = jnp.einsum(
        "blhd,bmhd->bhlm", query, keys, preferred_element_type=jnp.float32
    ) * hd ** (-0.5)
    mask = jnp.where(labels[:, :, None] == labels[:, None, :], 0.0, -100.0).astype(jnp.float32)
    scores = scores + rel_bias[None] + mask[:, None]
    scores = scores - jnp.max(scores, -1, keepdims=True)
    expo = jnp.exp(scores)
    probs = expo / jnp.sum(expo, -1, keepdims=True)
    return (query, keys, values, probs)


def attend_fwd(qkv, labels, rel_bias, heads):
    b, l, c3 = qkv.shape
    query, keys, values, probs = probabilities(qkv, labels, rel_bias, heads)
    probs_b = probs.astype(jnp.bfloat16)
    out = jnp.einsum("bhlm,bmhd->blhd", probs_b, values, preferred_element_type=jnp.float32)
    return out.astype(jnp.bfloat16).reshape(b, l, c3 // 3)


def attend_bwd(qkv, labels, rel_bias, grad_out, heads):
    b, l, c3 = qkv.shape
    c = c3 // 3
    hd = c // heads
    query, keys, values, probs = probabilities(qkv, labels, rel_bias, heads)
    probs_b = probs.astype(jnp.bfloat16)
    grad_heads = grad_out.reshape(b, l, heads, hd)
    d_val = jnp.einsum(
        "bhlm,blhd->bmhd", probs_b, grad_heads, preferred_element_type=jnp.float32
    ).astype(jnp.bfloat16)
    d_prob = jnp.einsum("blhd,bmhd->bhlm", grad_heads, values, preferred_element_type=jnp.float32)
    d_score = probs * (d_prob - jnp.sum(d_prob * probs, -1, keepdims=True))
    d_score = (d_score * hd ** (-0.5)).astype(jnp.bfloat16)
    d_query = jnp.einsum(
        "bhlm,bmhd->blhd", d_score, keys, preferred_element_type=jnp.float32
    ).astype(jnp.bfloat16)
    d_key = jnp.einsum(
        "bhlm,blhd->bmhd", d_score, query, preferred_element_type=jnp.float32
    ).astype(jnp.bfloat16)
    return jnp.concatenate(
        [d_query.reshape(b, l, c), d_key.reshape(b, l, c), d_val.reshape(b, l, c)], -1
    )


def blocked(func, arrays, per):
    count = arrays[0].shape[0]
    grouped = tuple((a.reshape((count // per, per) + a.shape[1:]) for a in arrays))
    result = lax.map(lambda items: func(*items), grouped)
    return result.reshape((count,) + result.shape[2:])


def shards(
    frames, cotangent, first_norm_gain, w_qkv, rel_bias, w_proj, second_norm_gain, w_up, w_down
):
    nfr, tile_h, tile_w, chan = frames.shape
    row_count = lax.axis_size("row")
    col_count = lax.axis_size("col")
    attention_residual_output, first_normalized_input, first_inverse_deviation = layer_norm_forward(
        frames, first_norm_gain
    )
    y_b = attention_residual_output.astype(jnp.bfloat16)
    shifted = split_windows(roll_ahead(y_b, SHIFT), WS)
    nwin, length, _ = shifted.shape
    flat_in = shifted.reshape(-1, chan)
    qkv = (
        jnp.dot(flat_in, w_qkv, preferred_element_type=jnp.float32)
        .astype(jnp.bfloat16)
        .reshape(nwin, length, 3 * chan)
    )
    row_lab = regions(lax.axis_index("row") * tile_h, tile_h, tile_h * row_count, WS, SHIFT)
    col_lab = regions(lax.axis_index("col") * tile_w, tile_w, tile_w * col_count, WS, SHIFT)
    grid = row_lab[:, None] * 3 + col_lab[None, :]
    labels = split_windows(jnp.broadcast_to(grid[None, :, :, None], (nfr, tile_h, tile_w, 1)), WS)[
        ..., 0
    ]
    per = math.gcd(nwin, max(1, 2048 // length))
    attended = blocked(lambda a, b: attend_fwd(a, b, rel_bias, HEADS), (qkv, labels), per).reshape(
        -1, chan
    )
    proj = jnp.dot(attended, w_proj, preferred_element_type=jnp.float32).astype(jnp.bfloat16)
    proj = merge_windows(proj.reshape(nwin, length, chan), nfr, tile_h, tile_w, WS)
    proj = roll_behind(proj, SHIFT)
    first_residual_input = (frames.astype(jnp.float32) + proj.astype(jnp.float32)).astype(
        jnp.bfloat16
    )
    block_final_output, second_normalized_input, second_inverse_deviation = layer_norm_forward(
        first_residual_input, second_norm_gain
    )
    z_b = block_final_output.astype(jnp.bfloat16).reshape(-1, chan)
    u_pre = jnp.dot(z_b, w_up, preferred_element_type=jnp.float32)
    act, slope = gelu_parts(u_pre)
    hid = act.astype(jnp.bfloat16)
    upstream_gradient = cotangent.reshape(-1, chan)
    g_down = jnp.dot(hid.T, upstream_gradient, preferred_element_type=jnp.float32)
    d_hid = jnp.dot(upstream_gradient, w_down.T, preferred_element_type=jnp.float32)
    d_up = (d_hid * slope).astype(jnp.bfloat16)
    g_up = jnp.dot(z_b.T, d_up, preferred_element_type=jnp.float32)
    residual_gradient = jnp.dot(d_up, w_up.T, preferred_element_type=jnp.float32).reshape(
        frames.shape
    )
    first_residual_gradient = cotangent.astype(jnp.float32) + layer_norm_backward(
        residual_gradient, second_norm_gain, second_normalized_input, second_inverse_deviation
    )
    dx_b = first_residual_gradient.astype(jnp.bfloat16)
    d_win = split_windows(roll_ahead(dx_b, SHIFT), WS).reshape(-1, chan)
    g_proj = jnp.dot(attended.T, d_win, preferred_element_type=jnp.float32)
    d_att = (
        jnp.dot(d_win, w_proj.T, preferred_element_type=jnp.float32)
        .astype(jnp.bfloat16)
        .reshape(nwin, length, chan)
    )
    d_qkv = blocked(
        lambda a, b, d: attend_bwd(a, b, rel_bias, d, HEADS), (qkv, labels, d_att), per
    ).reshape(-1, 3 * chan)
    g_qkv = jnp.dot(flat_in.T, d_qkv, preferred_element_type=jnp.float32)
    shifted_gradient = jnp.dot(d_qkv, w_qkv.T, preferred_element_type=jnp.float32).astype(
        jnp.bfloat16
    )
    shifted_gradient = merge_windows(
        shifted_gradient.reshape(nwin, length, chan), nfr, tile_h, tile_w, WS
    )
    shifted_gradient = roll_behind(shifted_gradient, SHIFT)
    frames_input_gradient = first_residual_gradient + layer_norm_backward(
        shifted_gradient.astype(jnp.float32),
        first_norm_gain,
        first_normalized_input,
        first_inverse_deviation,
    )
    g_down, g_up, g_proj, g_qkv = lax.psum((g_down, g_up, g_proj, g_qkv), ("row", "col"))
    factor = float(nfr * tile_h * tile_w * row_count * col_count) ** (-0.5)
    return (frames_input_gradient, g_qkv * factor, g_proj * factor, g_up * factor, g_down * factor)


def solution(mesh):
    placed = (
        P(None, "row", "col", None),
        P(None, "row", "col", None),
        P(),
        P(),
        P(),
        P(),
        P(),
        P(),
        P(),
    )
    return jax.shard_map(
        shards,
        mesh=mesh,
        in_specs=placed,
        out_specs=(P(None, "row", "col", None), P(), P(), P(), P()),
        check_vma=False,
    )
```

profile of v0, /device:TPU:1, one launch (start us, length us, event | category | flops | bytes accessed | tf_op | source)
XLA Modules:
  0.0 639.5 jit_solution(14623118505196249424)
XLA Ops:
  18.8 14.0 %collective-permute-done = bf16[16,32,8,128]{3,2,1,0:T(8,128)(2,1)} collective-permute-done((bf16[16,32,8,128]{3,2,1,0:T(8,128)(2,1)}, bf16[16,32,8,128]{3,2,1,0:T(8,128)(2,1)}, u32[]{:S(2)}, u32[]{:S(2)}) %collective-permute-start) | collective-permute-done | bytes 1048608 | tf_op jit(solution)/shard_map/ppermute | solution.py:19
  34.6 6.9 %collective-permute-start.1 = (bf16[16,8,16,128]{3,2,1,0:T(8,128)(2,1)}, bf16[16,8,16,128]{3,2,1,0:T(8,128)(2,1)}, u32[]{:S(2)}, u32[]{:S(2)}) collective-permute-start(bf16[16,8,16,128]{3,2,1,0:T(8,128)(2,1)} %pad_maximum_fusion.7), channel_id=1, source_target_pairs={{16,0},{32,16},{48,32},{64,48},{80,64},{96,80},{112,96},{0,112},{1... | collective-permute-start | bytes 1572872 | tf_op jit(solution)/shard_map/ppermute | solution.py:19
  46.4 5.0 collective-permute-done.1
  52.6 4.4 convolution_convert_fusion
  57.1 8.6 %copy.27 = bf16[4,8,256,384]{2,3,1,0:T(8,128)(2,1)} copy(bf16[4,8,256,384]{3,2,1,0:T(8,128)(2,1)} %bitcast.142) | data formatting | bytes 12582912 | tf_op jit(solution)/shard_map/while | solution.py:131
  65.6 70.5 %while.20 = (s32[]{:T(128)}, bf16[4,8,256,128]{3,2,1,0:T(8,128)(2,1)}, bf16[4,8,256,384]{2,3,1,0:T(8,128)(2,1)}, f32[4,256,256]{1,2,0:T(8,128)}, s32[4,8,256]{2,1,0:T(8,128)S(1)}, /*index=5*/s32[]{:T(128)}) while((s32[]{:T(128)}, bf16[4,8,256,128]{3,2,1,0:T(8,128)(2,1)}, bf16[4,8,256,384]{2,3,1,0:T(8,128)(2,1)}, f32[4,256,256]{1,2,0:T(8,128)}, ...), condition=%wide.region_5.6_spmd, body=%wide.region_2.5_spmd.sunk | while | flops 284426496 | bytes 32596056 | solution.py:131
  69.8 8.2 %fusion.155 = (f32[8,4,256]{2,1,0:T(4,128)S(1)}, f32[8,4,256,256]{2,3,1,0:T(8,128)}) fusion(f32[8,256,256]{1,2,0:T(8,128)} %compare_select_fusion.8, f32[4,256,256]{1,2,0:T(8,128)} %get-tuple-element.243, bf16[8,256,4,32]{1,3,2,0:T(8,128)(2,1)} %bitcast.158, bf16[8,256,4,32]{1,3,2,0:T(8,128)(2,1)S(1)} %bitcast.157), kind=kOutput, calls=%fused_computation.128.clone.1 | convolution fusion | flops 144703744 | bytes 12615680 | tf_op jit(solution)/shard_map/while/body/eval_jaxpr/sub | solution.py:90
  77.9 4.2 fusion.156
  87.4 8.2 %fusion.155 = (f32[8,4,256]{2,1,0:T(4,128)S(1)}, f32[8,4,256,256]{2,3,1,0:T(8,128)}) fusion(f32[8,256,256]{1,2,0:T(8,128)} %compare_select_fusion.8, f32[4,256,256]{1,2,0:T(8,128)} %get-tuple-element.243, bf16[8,256,4,32]{1,3,2,0:T(8,128)(2,1)} %bitcast.158, bf16[8,256,4,32]{1,3,2,0:T(8,128)(2,1)S(1)} %bitcast.157), kind=kOutput, calls=%fused_computation.128.clone.1 | convolution fusion | flops 144703744 | bytes 12615680 | tf_op jit(solution)/shard_map/while/body/eval_jaxpr/sub | solution.py:90
  95.5 4.2 fusion.156
  105.0 8.2 %fusion.155 = (f32[8,4,256]{2,1,0:T(4,128)S(1)}, f32[8,4,256,256]{2,3,1,0:T(8,128)}) fusion(f32[8,256,256]{1,2,0:T(8,128)} %compare_select_fusion.8, f32[4,256,256]{1,2,0:T(8,128)} %get-tuple-element.243, bf16[8,256,4,32]{1,3,2,0:T(8,128)(2,1)} %bitcast.158, bf16[8,256,4,32]{1,3,2,0:T(8,128)(2,1)S(1)} %bitcast.157), kind=kOutput, calls=%fused_computation.128.clone.1 | convolution fusion | flops 144703744 | bytes 12615680 | tf_op jit(solution)/shard_map/while/body/eval_jaxpr/sub | solution.py:90
  122.6 8.2 %fusion.155 = (f32[8,4,256]{2,1,0:T(4,128)S(1)}, f32[8,4,256,256]{2,3,1,0:T(8,128)}) fusion(f32[8,256,256]{1,2,0:T(8,128)} %compare_select_fusion.8, f32[4,256,256]{1,2,0:T(8,128)} %get-tuple-element.243, bf16[8,256,4,32]{1,3,2,0:T(8,128)(2,1)} %bitcast.158, bf16[8,256,4,32]{1,3,2,0:T(8,128)(2,1)S(1)} %bitcast.157), kind=kOutput, calls=%fused_computation.128.clone.1 | convolution fusion | flops 144703744 | bytes 12615680 | tf_op jit(solution)/shard_map/while/body/eval_jaxpr/sub | solution.py:90
  141.0 11.7 %collective-permute-done.2 = bf16[16,32,8,128]{3,2,1,0:T(8,128)(2,1)S(1)} collective-permute-done((bf16[16,32,8,128]{3,2,1,0:T(8,128)(2,1)S(1)}, bf16[16,32,8,128]{3,2,1,0:T(8,128)(2,1)S(1)}, u32[]{:S(2)}, u32[]{:S(2)}) %collective-permute-start.2) | collective-permute-done | bytes 1048608 | tf_op jit(solution)/shard_map/ppermute | solution.py:19
  154.7 14.7 %collective-permute-done.3 = bf16[16,8,16,128]{3,2,1,0:T(8,128)(2,1)} collective-permute-done((bf16[16,8,16,128]{3,2,1,0:T(8,128)(2,1)}, bf16[16,8,16,128]{3,2,1,0:T(8,128)(2,1)}, u32[]{:S(2)}, u32[]{:S(2)}) %collective-permute-start.3) | collective-permute-done | bytes 524320 | tf_op jit(solution)/shard_map/ppermute | solution.py:19
  179.4 8.7 %fusion.48 = bf16[8192,512]{1,0:T(8,128)(2,1)S(1)} fusion(f32[8192,512]{1,0:T(8,128)S(1)} %fusion.90, bf16[8192,128]{1,0:T(8,128)(2,1)S(1)} %bitcast.162, bf16[512,128]{1,0:T(8,128)(2,1)S(1)} %copy-done.46), kind=kOutput, calls=%fused_computation.53 | convolution fusion | flops 1115684864 | bytes 27394048 | tf_op jit(solution)/shard_map/dot_general | solution.py:178
  188.1 4.8 multiply_reduce_fusion.1
  193.1 6.9 %fusion.67 = f32[16,32,16]{2,1,0:T(8,128)S(1)} fusion(bf16[16,32,16,128]{3,2,1,0:T(8,128)(2,1)S(1)} %copy-done.5, f32[16,32,16,128]{3,2,1,0:T(8,128)} %bitcast.132, f32[128]{0:T(128)S(1)} %copy-done.42, f32[16,32,16]{2,1,0:T(8,128)S(1)} %add_rsqrt_fusion, f32[16,32,16]{2,1,0:T(8,128)S(1)} %broadcast_multiply_fusion.5), kind=kLoop, calls=%fused_computation.83 | loop fusion | flops 6283264 | bytes 6390272 | tf_op jit(solution)/shard_map/reduce_sum | solution.py:37
  200.7 4.9 fusion.79
  206.3 5.1 collective-permute-start.4
  211.4 5.2 fusion.49
  216.6 7.6 %collective-permute-done.4 = bf16[16,32,8,128]{3,2,1,0:T(8,128)(2,1)S(1)} collective-permute-done((bf16[16,32,8,128]{3,2,1,0:T(8,128)(2,1)S(1)}, bf16[16,32,8,128]{3,2,1,0:T(8,128)(2,1)S(1)}, u32[]{:S(2)}, u32[]{:S(2)}) %collective-permute-start.4) | collective-permute-done | bytes 1048608 | tf_op jit(solution)/shard_map/ppermute | solution.py:19
  228.4 7.8 %collective-permute-done.5 = bf16[16,8,16,128]{3,2,1,0:T(8,128)(2,1)S(1)} collective-permute-done((bf16[16,8,16,128]{3,2,1,0:T(8,128)(2,1)S(1)}, bf16[16,8,16,128]{3,2,1,0:T(8,128)(2,1)S(1)}, u32[]{:S(2)}, u32[]{:S(2)}) %collective-permute-start.5) | collective-permute-done | bytes 524320 | tf_op jit(solution)/shard_map/ppermute | solution.py:19
  239.7 194.2 %while.21 = (s32[]{:T(128)}, bf16[4,8,256,384]{3,2,1,0:T(8,128)(2,1)}, bf16[4,8,256,384]{2,3,1,0:T(8,128)(2,1)}, f32[4,256,256]{1,2,0:T(8,128)}, s32[4,8,256]{2,...) while((s32[]{:T(128)}, bf16[4,8,256,384]{3,2,1,0:T(8,128)(2,1)}, ...), condition=%wide.region_14.15_spmd, body=%wide.region_10.14_spmd.sunk | while | flops 721699584 | bytes 91381920 | solution.py:131
  244.0 7.7 %fusion.168 = (f32[8,4,256]{2,1,0:T(4,128)S(1)}, f32[8,4,256,256]{2,3,1,0:T(8,128)}) fusion(f32[8,256,256]{1,2,0:T(8,128)S(1)} %compare_select_fusion.9, f32[4,256,256]{1,2,0:T(8,128)} %get-tuple-element.263, bf16[8,256,4,32]{1,3,2,0:T(8,128)(2,1)} %bitcast.151, bf16[8,256,4,32]{1,3,2,0:T(8,128)(2,1)} %bitcast.153), kind=kOutput, calls=%fused_computation.130.clone.1 | convolution fusion | flops 144703744 | bytes 12615680 | tf_op jit(solution)/shard_map/while/body/eval_jaxpr/sub | solution.py:90
  251.7 4.7 fusion.169
  256.4 4.5 fusion.170
  261.0 13.0 %fusion.172 = bf16[8,4,32,256]{3,2,1,0:T(8,128)(2,1)S(1)} fusion(bf16[8,256,4,32]{1,3,2,0:T(8,128)(2,1)S(1)} %bitcast.154, f32[8,4,256,256]{2,3,1,0:T(8,128)} %fusion.170, f32[8,4,256,256]{2,3,1,0:T(8,128)} %get-tuple-element.225, f32[8,4,256]{2,1,0:T(4,128)S(1)} %get-tuple-element.226), kind=kOutput, calls=%fused_computation.36.clone.1 | convolution fusion | flops 149168384 | bytes 17858560 | tf_op jit(solution)/shard_map/while/body/eval_jaxpr/bhlm,bmhd->blhd/dot_general | solution.py:117
  274.0 11.9 %fusion.171 = bf16[8,4,32,256]{3,2,1,0:T(8,128)(2,1)S(1)} fusion(bf16[8,256,4,32]{1,3,2,0:T(8,128)(2,1)S(1)} %bitcast.152, f32[8,4,256,256]{2,3,1,0:T(8,128)} %fusion.170, f32[8,4,256,256]{2,3,1,0:T(8,128)} %get-tuple-element.225, f32[8,4,256]{2,1,0:T(4,128)S(1)} %get-tuple-element.226), kind=kOutput, calls=%fused_computation.37.clone.1 | convolution fusion | flops 149168384 | bytes 17858560 | tf_op jit(solution)/shard_map/while/body/eval_jaxpr/bhlm,blhd->bmhd/dot_general | solution.py:120
  292.5 7.7 %fusion.168 = (f32[8,4,256]{2,1,0:T(4,128)S(1)}, f32[8,4,256,256]{2,3,1,0:T(8,128)}) fusion(f32[8,256,256]{1,2,0:T(8,128)S(1)} %compare_select_fusion.9, f32[4,256,256]{1,2,0:T(8,128)} %get-tuple-element.263, bf16[8,256,4,32]{1,3,2,0:T(8,128)(2,1)} %bitcast.151, bf16[8,256,4,32]{1,3,2,0:T(8,128)(2,1)} %bitcast.153), kind=kOutput, calls=%fused_computation.130.clone.1 | convolution fusion | flops 144703744 | bytes 12615680 | tf_op jit(solution)/shard_map/while/body/eval_jaxpr/sub | solution.py:90
  300.2 4.7 fusion.169
  304.9 4.5 fusion.170
  309.5 13.0 %fusion.172 = bf16[8,4,32,256]{3,2,1,0:T(8,128)(2,1)S(1)} fusion(bf16[8,256,4,32]{1,3,2,0:T(8,128)(2,1)S(1)} %bitcast.154, f32[8,4,256,256]{2,3,1,0:T(8,128)} %fusion.170, f32[8,4,256,256]{2,3,1,0:T(8,128)} %get-tuple-element.225, f32[8,4,256]{2,1,0:T(4,128)S(1)} %get-tuple-element.226), kind=kOutput, calls=%fused_computation.36.clone.1 | convolution fusion | flops 149168384 | bytes 17858560 | tf_op jit(solution)/shard_map/while/body/eval_jaxpr/bhlm,bmhd->blhd/dot_general | solution.py:117
  322.5 11.9 %fusion.171 = bf16[8,4,32,256]{3,2,1,0:T(8,128)(2,1)S(1)} fusion(bf16[8,256,4,32]{1,3,2,0:T(8,128)(2,1)S(1)} %bitcast.152, f32[8,4,256,256]{2,3,1,0:T(8,128)} %fusion.170, f32[8,4,256,256]{2,3,1,0:T(8,128)} %get-tuple-element.225, f32[8,4,256]{2,1,0:T(4,128)S(1)} %get-tuple-element.226), kind=kOutput, calls=%fused_computation.37.clone.1 | convolution fusion | flops 149168384 | bytes 17858560 | tf_op jit(solution)/shard_map/while/body/eval_jaxpr/bhlm,blhd->bmhd/dot_general | solution.py:120
  341.0 7.7 %fusion.168 = (f32[8,4,256]{2,1,0:T(4,128)S(1)}, f32[8,4,256,256]{2,3,1,0:T(8,128)}) fusion(f32[8,256,256]{1,2,0:T(8,128)S(1)} %compare_select_fusion.9, f32[4,256,256]{1,2,0:T(8,128)} %get-tuple-element.263, bf16[8,256,4,32]{1,3,2,0:T(8,128)(2,1)} %bitcast.151, bf16[8,256,4,32]{1,3,2,0:T(8,128)(2,1)} %bitcast.153), kind=kOutput, calls=%fused_computation.130.clone.1 | convolution fusion | flops 144703744 | bytes 12615680 | tf_op jit(solution)/shard_map/while/body/eval_jaxpr/sub | solution.py:90
  348.7 4.7 fusion.169
  353.4 4.5 fusion.170
  357.9 13.0 %fusion.172 = bf16[8,4,32,256]{3,2,1,0:T(8,128)(2,1)S(1)} fusion(bf16[8,256,4,32]{1,3,2,0:T(8,128)(2,1)S(1)} %bitcast.154, f32[8,4,256,256]{2,3,1,0:T(8,128)} %fusion.170, f32[8,4,256,256]{2,3,1,0:T(8,128)} %get-tuple-element.225, f32[8,4,256]{2,1,0:T(4,128)S(1)} %get-tuple-element.226), kind=kOutput, calls=%fused_computation.36.clone.1 | convolution fusion | flops 149168384 | bytes 17858560 | tf_op jit(solution)/shard_map/while/body/eval_jaxpr/bhlm,bmhd->blhd/dot_general | solution.py:117
  370.9 11.9 %fusion.171 = bf16[8,4,32,256]{3,2,1,0:T(8,128)(2,1)S(1)} fusion(bf16[8,256,4,32]{1,3,2,0:T(8,128)(2,1)S(1)} %bitcast.152, f32[8,4,256,256]{2,3,1,0:T(8,128)} %fusion.170, f32[8,4,256,256]{2,3,1,0:T(8,128)} %get-tuple-element.225, f32[8,4,256]{2,1,0:T(4,128)S(1)} %get-tuple-element.226), kind=kOutput, calls=%fused_computation.37.clone.1 | convolution fusion | flops 149168384 | bytes 17858560 | tf_op jit(solution)/shard_map/while/body/eval_jaxpr/bhlm,blhd->bmhd/dot_general | solution.py:120
  389.5 7.7 %fusion.168 = (f32[8,4,256]{2,1,0:T(4,128)S(1)}, f32[8,4,256,256]{2,3,1,0:T(8,128)}) fusion(f32[8,256,256]{1,2,0:T(8,128)S(1)} %compare_select_fusion.9, f32[4,256,256]{1,2,0:T(8,128)} %get-tuple-element.263, bf16[8,256,4,32]{1,3,2,0:T(8,128)(2,1)} %bitcast.151, bf16[8,256,4,32]{1,3,2,0:T(8,128)(2,1)} %bitcast.153), kind=kOutput, calls=%fused_computation.130.clone.1 | convolution fusion | flops 144703744 | bytes 12615680 | tf_op jit(solution)/shard_map/while/body/eval_jaxpr/sub | solution.py:90
  397.2 4.7 fusion.169
  401.9 4.5 fusion.170
  406.4 13.0 %fusion.172 = bf16[8,4,32,256]{3,2,1,0:T(8,128)(2,1)S(1)} fusion(bf16[8,256,4,32]{1,3,2,0:T(8,128)(2,1)S(1)} %bitcast.154, f32[8,4,256,256]{2,3,1,0:T(8,128)} %fusion.170, f32[8,4,256,256]{2,3,1,0:T(8,128)} %get-tuple-element.225, f32[8,4,256]{2,1,0:T(4,128)S(1)} %get-tuple-element.226), kind=kOutput, calls=%fused_computation.36.clone.1 | convolution fusion | flops 149168384 | bytes 17858560 | tf_op jit(solution)/shard_map/while/body/eval_jaxpr/bhlm,bmhd->blhd/dot_general | solution.py:117
  419.4 11.9 %fusion.171 = bf16[8,4,32,256]{3,2,1,0:T(8,128)(2,1)S(1)} fusion(bf16[8,256,4,32]{1,3,2,0:T(8,128)(2,1)S(1)} %bitcast.152, f32[8,4,256,256]{2,3,1,0:T(8,128)} %fusion.170, f32[8,4,256,256]{2,3,1,0:T(8,128)} %get-tuple-element.225, f32[8,4,256]{2,1,0:T(4,128)S(1)} %get-tuple-element.226), kind=kOutput, calls=%fused_computation.37.clone.1 | convolution fusion | flops 149168384 | bytes 17858560 | tf_op jit(solution)/shard_map/while/body/eval_jaxpr/bhlm,blhd->bmhd/dot_general | solution.py:120
  434.0 4.7 convolution_convert_fusion.1
  446.6 148.0 %all-reduce.3.cloned.1.call-done = (f32[128,384]{1,0:T(8,128)}, f32[128,128]{1,0:T(8,128)}, f32[128,512]{1,0:T(8,128)}, f32[512,128]{1,0:T(8,128)}) async-done(((f32[128,384]{1,0:T(8,128)}, f32[128,128]{1,0:T(8,128)}, f32[128,512]{1,0:T(8,128)}, f32[512,128]{1,0:T(8,128)}), (f32[128,384]{1,0:T(8,128)}, f32[128,128]{1,0:T(8,128)}, f32[128,512]{1,0:T(8,128)}, ...) | async-done | bytes 786448 | tf_op jit(solution)/shard_map/psum | solution.py:212
  603.9 9.7 %collective-permute-done.7 = bf16[16,8,16,128]{3,2,1,0:T(8,128)(2,1)S(1)} collective-permute-done((bf16[16,8,16,128]{3,2,1,0:T(8,128)(2,1)S(1)}, bf16[16,8,16,128]{3,2,1,0:T(8,128)(2,1)S(1)}, u32[]{:S(2)}, u32[]{:S(2)}) %collective-permute-start.7) | collective-permute-done | bytes 524320 | tf_op jit(solution)/shard_map/ppermute | solution.py:19
  613.6 6.8 %fusion.73 = (f32[16,32,16]{2,1,0:T(8,128)S(1)}, f32[16,32,16]{2,1,0:T(8,128)S(1)}) fusion(f32[128]{0:T(128)S(1)} %copy-done.45, bf16[16,32,8,128]{3,2,1,0:T(8,128)(2,1)S(1)} %get-tuple-element.129, bf16[16,32,8,128]{3,2,1,0:T(8,128)(2,1)} %collective-permute-done.6, bf16[16,8,16,128]{3,2,1,0:T(8,128)(2,1)S(1)} %collective-permute-done.7, ...), kind=kLoop, calls=%fused_computation.90 | loop fusion | flops 13615104 | bytes 4850176 | tf_op jit(solution)/shard_map/reduce_sum | solution.py:36
  620.6 11.7 %fusion.64 = f32[16,32,16,128]{3,2,1,0:T(8,128)} fusion(bf16[16,32,16,128]{3,2,1,0:T(8,128)(2,1)S(1)} %copy-done.3, f32[16,32,16]{2,1,0:T(8,128)S(1)} %get-tuple-element.138, f32[16,32,16]{2,1,0:T(8,128)S(1)} %get-tuple-element.139, f32[128]{0:T(128)S(1)} %copy-done.45, f32[16,32,16]{2,1,0:T(8,128)S(1)} %copy-done.32, f32[16,32,16]{2,1,0:T(8,128)S(1)} %copy-done.30, ...), kind=kLoop, calls=%fused_computation.80 | loop fusion | flops 26214400 | bytes 17564672 | tf_op jit(solution)/shard_map/add | solution.py:206
  (226 shorter events, 118.0 us)
Async XLA Ops:
  7.2 169.8 %copy-start = (bf16[128,512]{1,0:T(8,128)(2,1)S(1)}, bf16[128,512]{1,0:T(8,128)(2,1)}, u32[]{:S(2)}) copy-start(bf16[128,512]{1,0:T(8,128)(2,1)} %param.20) | copy-start | bytes 393220
  7.2 6.2 copy-start.44
  7.2 587.5 %all-reduce.3.cloned.1.call-start = ((), (), s32[]{:S(2)}) async-start(), calls=%async_computation | async-start | bytes 1572864 | tf_op jit(solution)/shard_map/psum | solution.py:212
  17.4 15.4 %collective-permute-start = (bf16[16,32,8,128]{3,2,1,0:T(8,128)(2,1)}, bf16[16,32,8,128]{3,2,1,0:T(8,128)(2,1)}, u32[]{:S(2)}, u32[]{:S(2)}) collective-permute-start(bf16[16,32,8,128]{3,2,1,0:T(8,128)(2,1)} %get-tuple-element.135), channel_id=1, source_target_pairs={{1,0},{2,1},{3,2},{4,3},{5,4},{6,5},{7,6},{8,7},{9,8},{10,9},{11,1... | collective-permute-start | bytes 3145736 | tf_op jit(solution)/shard_map/ppermute | solution.py:19
  34.6 16.8 %collective-permute-start.1 = (bf16[16,8,16,128]{3,2,1,0:T(8,128)(2,1)}, bf16[16,8,16,128]{3,2,1,0:T(8,128)(2,1)}, u32[]{:S(2)}, u32[]{:S(2)}) collective-permute-start(bf16[16,8,16,128]{3,2,1,0:T(8,128)(2,1)} %pad_maximum_fusion.7), channel_id=1, source_target_pairs={{16,0},{32,16},{48,32},{64,48},{80,64},{96,80},{112,96},{0,112},{1... | collective-permute-start | bytes 1572872 | tf_op jit(solution)/shard_map/ppermute | solution.py:19
  44.9 7.7 %copy-start.39 = (bf16[128,384]{1,0:T(8,128)(2,1)S(1)}, bf16[128,384]{1,0:T(8,128)(2,1)}, u32[]{:S(2)}) copy-start(bf16[128,384]{1,0:T(8,128)(2,1)} %param.16) | copy-start | bytes 294916
  57.1 8.6 %copy-start.38 = (s32[4,8,256]{2,1,0:T(8,128)S(1)}, s32[4,8,256]{2,1,0:T(8,128)}, u32[]{:S(2)}) copy-start(s32[4,8,256]{2,1,0:T(8,128)} %broadcast_in_dim.95) | copy-start | bytes 98308
  65.6 70.5 %copy-start.41 = (bf16[128,128]{1,0:T(8,128)(2,1)S(1)}, bf16[128,128]{1,0:T(8,128)(2,1)}, u32[]{:S(2)}) copy-start(bf16[128,128]{1,0:T(8,128)(2,1)} %param.18) | copy-start | bytes 98308
  138.8 13.9 %collective-permute-start.2 = (bf16[16,32,8,128]{3,2,1,0:T(8,128)(2,1)S(1)}, bf16[16,32,8,128]{3,2,1,0:T(8,128)(2,1)S(1)}, u32[]{:S(2)}, u32[]{:S(2)}) collective-permute-start(bf16[16,32,8,128]{3,2,1,0:T(8,128)(2,1)S(1)} %get-tuple-element.132), channel_id=1, source_target_pairs={{15,0},{0,1},{1,2},{2,3},{3,4},{4,5},{5,6},{6,7},{7,8},{8,9},{9,10... | collective-permute-start | bytes 3145736 | tf_op jit(solution)/shard_map/ppermute | solution.py:19
  154.6 14.9 %collective-permute-start.3 = (bf16[16,8,16,128]{3,2,1,0:T(8,128)(2,1)}, bf16[16,8,16,128]{3,2,1,0:T(8,128)(2,1)}, u32[]{:S(2)}, u32[]{:S(2)}) collective-permute-start(bf16[16,8,16,128]{3,2,1,0:T(8,128)(2,1)} %pad_maximum_fusion.6), channel_id=1, source_target_pairs={{112,0},{0,16},{16,32},{32,48},{48,64},{64,80},{80,96},{96,112},{1... | collective-permute-start | bytes 1572872 | tf_op jit(solution)/shard_map/ppermute | solution.py:19
  154.7 19.7 %copy-start.42 = (f32[128]{0:T(128)S(1)}, f32[128]{0:T(128)}, u32[]{:S(2)}) copy-start(f32[128]{0:T(128)} %param.19) | copy-start | bytes 1540
  171.9 5.1 copy-start.4
  172.0 28.0 %copy-start.22 = (f32[16,32,16]{2,1,0:T(8,128)}, f32[16,32,16]{2,1,0:T(8,128)S(1)}, u32[]{:S(2)}) copy-start(f32[16,32,16]{2,1,0:T(8,128)S(1)} %broadcast_multiply_fusion.5) | copy-start | bytes 98308
  174.5 25.5 %copy-start.27 = (f32[16,32,16]{2,1,0:T(8,128)}, f32[16,32,16]{2,1,0:T(8,128)S(1)}, u32[]{:S(2)}) copy-start(f32[16,32,16]{2,1,0:T(8,128)S(1)} %add_rsqrt_fusion) | copy-start | bytes 98308
  179.4 8.7 %copy-start.17 = (f32[8192,512]{1,0:T(8,128)}, f32[8192,512]{1,0:T(8,128)S(1)}, u32[]{:S(2)}) copy-start(f32[8192,512]{1,0:T(8,128)S(1)} %fusion.90) | copy-start | bytes 50331652
  188.1 5.0 copy-start.5
  193.0 12.6 %copy-start.34 = (f32[16,32,16]{2,1,0:T(8,128)}, f32[16,32,16]{2,1,0:T(8,128)S(1)}, u32[]{:S(2)}) copy-start(f32[16,32,16]{2,1,0:T(8,128)S(1)} %div.47) | copy-start | bytes 98308
  193.0 7.7 %copy-start.7 = (f32[8192,128]{1,0:T(8,128)S(1)}, f32[8192,128]{1,0:T(8,128)}, u32[]{:S(2)}) copy-start(f32[8192,128]{1,0:T(8,128)} %get-tuple-element.137) | copy-start | bytes 12582916
  193.1 7.7 %copy-start.25 = (bf16[16,32,16,128]{3,2,1,0:T(8,128)(2,1)S(1)}, bf16[16,32,16,128]{3,2,1,0:T(8,128)(2,1)}, u32[]{:S(2)}) copy-start(bf16[16,32,16,128]{3,2,1,0:T(8,128)(2,1)} %param.14) | copy-start | bytes 6291460
  193.1 18.3 %copy-start.18 = (f32[8192,512]{1,0:T(8,128)S(1)}, f32[8192,512]{1,0:T(8,128)}, u32[]{:S(2)}) copy-start(f32[8192,512]{1,0:T(8,128)} %copy-done.17) | copy-start | bytes 50331652
  206.3 19.8 %slice-start = ((s8[8388608]{0:T(1024)(128)(4,1)}), s8[4194304]{0:T(1024)(128)(4,1)S(1)}, s32[]{:S(2)}) async-start(s8[8388608]{0:T(1024)(128)(4,1)} %bitcast.133), calls=%async_computation.1 | async-start | bytes 8388608
  206.3 19.8 %slice-start.1 = ((s8[8388608]{0:T(1024)(128)(4,1)}), s8[4194304]{0:T(1024)(128)(4,1)S(1)}, s32[]{:S(2)}) async-start(s8[8388608]{0:T(1024)(128)(4,1)} %bitcast.133), calls=%async_computation.2 | async-start | bytes 8388608
  206.3 19.8 %copy-start.14 = (bf16[16,32,16,128]{3,2,1,0:T(8,128)(2,1)S(1)}, bf16[16,32,16,128]{3,2,1,0:T(8,128)(2,1)}, u32[]{:S(2)}) copy-start(bf16[16,32,16,128]{3,2,1,0:T(8,128)(2,1)} %copy-done.13) | copy-start | bytes 6291460
  206.3 18.0 %collective-permute-start.4 = (bf16[16,32,8,128]{3,2,1,0:T(8,128)(2,1)S(1)}, bf16[16,32,8,128]{3,2,1,0:T(8,128)(2,1)S(1)}, u32[]{:S(2)}, u32[]{:S(2)}) collective-permute-start(bf16[16,32,8,128]{3,2,1,0:T(8,128)(2,1)S(1)} %get-tuple-element.131), channel_id=1, source_target_pairs={{1,0},{2,1},{3,2},{4,3},{5,4},{6,5},{7,6},{8,7},{9,8},{10,9},{11,1... | collective-permute-start | bytes 3145736 | tf_op jit(solution)/shard_map/ppermute | solution.py:19
  224.4 11.8 %collective-permute-start.5 = (bf16[16,8,16,128]{3,2,1,0:T(8,128)(2,1)S(1)}, bf16[16,8,16,128]{3,2,1,0:T(8,128)(2,1)S(1)}, u32[]{:S(2)}, u32[]{:S(2)}) collective-permute-start(bf16[16,8,16,128]{3,2,1,0:T(8,128)(2,1)S(1)} %pad_maximum_fusion.5), channel_id=1, source_target_pairs={{16,0},{32,16},{48,32},{64,48},{80,64},{96,80},{112,96},{0,112},{1... | collective-permute-start | bytes 1572872 | tf_op jit(solution)/shard_map/ppermute | solution.py:19
  239.7 194.2 %copy-start.40 = (bf16[128,384]{1,0:T(8,128)(2,1)S(1)}, bf16[128,384]{1,0:T(8,128)(2,1)}, u32[]{:S(2)}) copy-start(bf16[128,384]{1,0:T(8,128)(2,1)} %param.16) | copy-start | bytes 294916
  261.0 13.0 %copy-start.20 = (bf16[8,256,128]{1,2,0:T(8,128)(2,1)S(1)}, bf16[8,256,128]{1,2,0:T(8,128)(2,1)}, u32[]{:S(2)}) copy-start(bf16[8,256,128]{1,2,0:T(8,128)(2,1)} %get-tuple-element.223) | copy-start | bytes 1572868 | tf_op jit(solution)/shard_map/while
  309.5 13.0 %copy-start.20 = (bf16[8,256,128]{1,2,0:T(8,128)(2,1)S(1)}, bf16[8,256,128]{1,2,0:T(8,128)(2,1)}, u32[]{:S(2)}) copy-start(bf16[8,256,128]{1,2,0:T(8,128)(2,1)} %get-tuple-element.223) | copy-start | bytes 1572868 | tf_op jit(solution)/shard_map/while
  357.9 13.0 %copy-start.20 = (bf16[8,256,128]{1,2,0:T(8,128)(2,1)S(1)}, bf16[8,256,128]{1,2,0:T(8,128)(2,1)}, u32[]{:S(2)}) copy-start(bf16[8,256,128]{1,2,0:T(8,128)(2,1)} %get-tuple-element.223) | copy-start | bytes 1572868 | tf_op jit(solution)/shard_map/while
  406.4 13.0 %copy-start.20 = (bf16[8,256,128]{1,2,0:T(8,128)(2,1)S(1)}, bf16[8,256,128]{1,2,0:T(8,128)(2,1)}, u32[]{:S(2)}) copy-start(bf16[8,256,128]{1,2,0:T(8,128)(2,1)} %get-tuple-element.223) | copy-start | bytes 1572868 | tf_op jit(solution)/shard_map/while
  434.0 9.2 %copy-start.10 = (bf16[4,8,256,384]{3,2,1,0:T(8,128)(2,1)S(1)}, bf16[4,8,256,384]{3,2,1,0:T(8,128)(2,1)}, u32[]{:S(2)}) copy-start(bf16[4,8,256,384]{3,2,1,0:T(8,128)(2,1)} %get-tuple-element.65) | copy-start | bytes 18874372
  440.3 4.9 copy-start.16
  440.3 4.9 copy-start.19
  440.3 156.1 %collective-permute-start.6 = (bf16[16,32,8,128]{3,2,1,0:T(8,128)(2,1)}, bf16[16,32,8,128]{3,2,1,0:T(8,128)(2,1)}, u32[]{:S(2)}, u32[]{:S(2)}) collective-permute-start(bf16[16,32,8,128]{3,2,1,0:T(8,128)(2,1)} %get-tuple-element.128), channel_id=1, source_target_pairs={{15,0},{0,1},{1,2},{2,3},{3,4},{4,5},{5,6},{6,7},{7,8},{8,9},{9,10... | collective-permute-start | bytes 3145736 | tf_op jit(solution)/shard_map/ppermute | solution.py:19
  445.2 168.4 %copy-start.3 = (bf16[16,32,16,128]{3,2,1,0:T(8,128)(2,1)S(1)}, bf16[16,32,16,128]{3,2,1,0:T(8,128)(2,1)}, u32[]{:S(2)}) copy-start(bf16[16,32,16,128]{3,2,1,0:T(8,128)(2,1)} %param.13) | copy-start | bytes 6291460
  445.2 168.4 %copy-start.30 = (f32[16,32,16]{2,1,0:T(8,128)S(1)}, f32[16,32,16]{2,1,0:T(8,128)}, u32[]{:S(2)}) copy-start(f32[16,32,16]{2,1,0:T(8,128)} %copy-done.29) | copy-start | bytes 98308
  445.2 168.4 %copy-start.45 = (f32[128]{0:T(128)S(1)}, f32[128]{0:T(128)}, u32[]{:S(2)}) copy-start(f32[128]{0:T(128)} %param.15) | copy-start | bytes 1540
  594.7 18.9 %copy-start.32 = (f32[16,32,16]{2,1,0:T(8,128)S(1)}, f32[16,32,16]{2,1,0:T(8,128)}, u32[]{:S(2)}) copy-start(f32[16,32,16]{2,1,0:T(8,128)} %copy-done.31) | copy-start | bytes 98308
  596.3 24.2 %copy-start.26 = (bf16[16,32,16,128]{3,2,1,0:T(8,128)(2,1)S(1)}, bf16[16,32,16,128]{3,2,1,0:T(8,128)(2,1)}, u32[]{:S(2)}) copy-start(bf16[16,32,16,128]{3,2,1,0:T(8,128)(2,1)} %param.14) | copy-start | bytes 6291460
  597.5 23.0 %copy-start.6 = (bf16[16,32,16,128]{3,2,1,0:T(8,128)(2,1)S(1)}, bf16[16,32,16,128]{3,2,1,0:T(8,128)(2,1)}, u32[]{:S(2)}) copy-start(bf16[16,32,16,128]{3,2,1,0:T(8,128)(2,1)} %copy-done.4) | copy-start | bytes 6291460
  597.6 23.0 %copy-start.8 = (f32[8192,128]{1,0:T(8,128)S(1)}, f32[8192,128]{1,0:T(8,128)}, u32[]{:S(2)}) copy-start(f32[8192,128]{1,0:T(8,128)} %get-tuple-element.137) | copy-start | bytes 12582916
  597.6 23.0 %copy-start.23 = (f32[16,32,16]{2,1,0:T(8,128)S(1)}, f32[16,32,16]{2,1,0:T(8,128)}, u32[]{:S(2)}) copy-start(f32[16,32,16]{2,1,0:T(8,128)} %copy-done.22) | copy-start | bytes 98308
  597.6 23.0 %copy-start.28 = (f32[16,32,16]{2,1,0:T(8,128)S(1)}, f32[16,32,16]{2,1,0:T(8,128)}, u32[]{:S(2)}) copy-start(f32[16,32,16]{2,1,0:T(8,128)} %copy-done.27) | copy-start | bytes 98308
  597.6 23.0 %copy-start.35 = (f32[16,32,16]{2,1,0:T(8,128)S(1)}, f32[16,32,16]{2,1,0:T(8,128)}, u32[]{:S(2)}) copy-start(f32[16,32,16]{2,1,0:T(8,128)} %copy-done.34) | copy-start | bytes 98308
  597.6 23.0 %copy-start.37 = (f32[16,32,16]{2,1,0:T(8,128)S(1)}, f32[16,32,16]{2,1,0:T(8,128)}, u32[]{:S(2)}) copy-start(f32[16,32,16]{2,1,0:T(8,128)} %copy-done.36) | copy-start | bytes 98308
  597.6 23.0 %copy-start.43 = (f32[128]{0:T(128)S(1)}, f32[128]{0:T(128)}, u32[]{:S(2)}) copy-start(f32[128]{0:T(128)} %param.19) | copy-start | bytes 1540
  597.6 15.9 %collective-permute-start.7 = (bf16[16,8,16,128]{3,2,1,0:T(8,128)(2,1)S(1)}, bf16[16,8,16,128]{3,2,1,0:T(8,128)(2,1)S(1)}, u32[]{:S(2)}, u32[]{:S(2)}) collective-permute-start(bf16[16,8,16,128]{3,2,1,0:T(8,128)(2,1)S(1)} %pad_maximum_fusion.4), channel_id=1, source_target_pairs={{112,0},{0,16},{16,32},{32,48},{48,64},{64,80},{80,96},{96,112},{1... | collective-permute-start | bytes 1572872 | tf_op jit(solution)/shard_map/ppermute | solution.py:19
  620.6 11.8 %copy-start.1 = (bf16[128,512]{1,0:T(8,128)(2,1)S(1)}, bf16[128,512]{1,0:T(8,128)(2,1)}, u32[]{:S(2)}) copy-start(bf16[128,512]{1,0:T(8,128)(2,1)} %param.20) | copy-start | bytes 393220
  (16 other events, 48.2 us)
Sparse Core Ops, SparseCore 0:
  446.8 147.8 all-reduce.2
where the time goes:
time: 645 us; the launch traced here: 639 us
  matrix products  257 us (40%)
  waiting for transfers between devices  219 us (34%)
  other arithmetic  68.2 us (11%)
  local copies, waits for them, and re-layouts  58.8 us (9%)
  starting transfers between devices  21.3 us (3%)
  between operations  15 us (2%)
    psum x1, waiting for transfers between devices, shards(): lax.psum((g_down, g_up, g_proj, g_qkv), ('row', 'col'))  148 us
    ppermute x8, waiting for transfers between devices, from_behind(): return lax.ppermute(block, axis, route)  70.5 us
    sub x8, matrix products, probabilities(): scores = scores - jnp.max(scores, -1, keepdims=True)  63.4 us
    dot_general x4, matrix products, attend_bwd(): jnp.einsum('bhlm,bmhd->blhd', d_score, keys, preferred_element_type=jnp.f...  51.9 us
    dot_general x4, matrix products, attend_bwd(): jnp.einsum('bhlm,blhd->bmhd', d_score, query, preferred_element_type=jnp....  47.8 us
    ppermute x8, starting transfers between devices, from_behind(): return lax.ppermute(block, axis, route)  21.3 us
    dot_general x4, matrix products, attend_bwd(): jnp.einsum('bhlm,blhd->bmhd', probs_b, grad_heads, preferred_element_type...  18.8 us
    dot_general x4, matrix products, attend_bwd(): jnp.einsum('blhd,bmhd->bhlm', grad_heads, values, preferred_element_type=...  18.1 us
  transfers between devices with their start and end apart: 9, of which 8 were waited for; matrix products, arithmetic and copies ran while one was open for 4% of the time, Pallas kernels for 0%

commit v1 on v0

v1 whole, which is shorter than its diff:
```python
import functools
import math

import jax
import jax.numpy as jnp
from jax import lax
from jax.experimental import pallas as pl
from jax.experimental.pallas import tpu as pltpu
from jax.sharding import PartitionSpec as P

HEADS = 4
WS = 16
SHIFT = 8
EPS = 1e-05
LOG2E = math.log2(math.e)
MESH = pl.DeviceIdType.MESH
bf16 = jnp.bfloat16
f32 = jnp.float32


def dot(a, b, ca, cb):
    return lax.dot_general(a, b, (((ca,), (cb,)), ((), ())), preferred_element_type=f32)


def layer_norm_stats(x):
    centered = x - jnp.mean(x, -1, keepdims=True)
    rstd = lax.rsqrt(jnp.mean(centered * centered, -1, keepdims=True) + EPS)
    return centered * rstd, rstd


def layer_norm_backward(dy, gain, xhat, rstd):
    dxh = dy * gain
    return rstd * (
        dxh
        - jnp.mean(dxh, -1, keepdims=True)
        - xhat * jnp.mean(dxh * xhat, -1, keepdims=True)
    )


def gelu_and_slope(u):
    expo = jnp.exp2(u * u * (-0.5 * LOG2E))
    t = 1.0 / (1.0 + (0.3275911 / math.sqrt(2.0)) * jnp.abs(u))
    poly = 0.5 * 1.061405429
    for c in (-1.453152027, 1.421413741, -0.284496736, 0.254829592):
        poly = t * poly + 0.5 * c
    tail = t * poly * expo
    cdf = jnp.where(u < 0.0, tail, 1.0 - tail)
    return u * cdf, cdf + u * expo * (1.0 / math.sqrt(2.0 * math.pi))


def window_block(x, c, w, g1, g2, w_qkv, w_proj, w_up, w_down, bias, probs, acc):
    gq, gp, gu, gd = acc
    tokens, chan = x.shape
    hd = chan // HEADS
    head = lax.broadcasted_iota(jnp.int32, (tokens, chan), 1) // hd
    xhat1, rstd1 = layer_norm_stats(x)
    y = (xhat1 * g1).astype(bf16)
    qkv = dot(y, w_qkv[...], 1, 0)
    q = qkv[:, :chan] * (LOG2E / math.sqrt(hd))
    k = qkv[:, chan : 2 * chan].astype(bf16)
    v_one = jnp.concatenate([qkv[:, 2 * chan :].astype(bf16), jnp.ones((tokens, chan), bf16)], 1)
    total, norm = None, None
    for h in range(HEADS):
        mine = head == h
        scores = dot(jnp.where(mine, q, 0.0).astype(bf16), k, 1, 1) + bias[w, h]
        expo = jnp.exp2(scores - jnp.max(scores, -1, keepdims=True)).astype(bf16)
        probs[w, h] = expo
        out = dot(expo, v_one, 1, 0)
        total = out[:, :chan] if h == 0 else jnp.where(mine, out[:, :chan], total)
        norm = out[:, chan:] if h == 0 else jnp.where(mine, out[:, chan:], norm)
    inverse = 1.0 / norm
    attended = total * inverse
    attended_b = attended.astype(bf16)
    proj = dot(attended_b, w_proj[...], 1, 0).astype(bf16)
    x1 = (x + proj.astype(f32)).astype(bf16).astype(f32)
    xhat2, rstd2 = layer_norm_stats(x1)
    z = (xhat2 * g2).astype(bf16)
    c_b = c.astype(bf16)
    act, slope = gelu_and_slope(dot(z, w_up[...], 1, 0))
    hid = act.astype(bf16)
    du = (dot(c_b, w_down[...], 1, 1) * slope).astype(bf16)
    gd[...] += dot(c_b, hid, 0, 0)
    gu[...] += dot(z, du, 0, 0)
    dx1 = c + layer_norm_backward(dot(du, w_up[...], 1, 1), g2, xhat2, rstd2)
    dx1_b = dx1.astype(bf16)
    gp[...] += dot(attended_b, dx1_b, 0, 0)
    d_att = dot(dx1_b, w_proj[...], 1, 1).astype(bf16).astype(f32) * inverse
    d_sum = -(d_att * attended)
    q_t = q.astype(bf16).T
    d_att_t = d_att.astype(bf16).T
    dv, dk, dq = [], [], None
    for h in range(HEADS):
        mine = head == h
        left = jnp.concatenate(
            [jnp.where(mine, d_att, 0.0).astype(bf16), jnp.where(mine, d_sum, 0.0).astype(bf16)], 1
        )
        expo = probs[w, h]
        ds = (expo.astype(f32) * dot(left, v_one, 1, 1)).astype(bf16)
        dv.append(dot(d_att_t[hd * h : hd * (h + 1)], expo, 1, 0))
        dk.append(dot(q_t[hd * h : hd * (h + 1)], ds, 1, 0))
        out = dot(ds, k, 1, 0)
        dq = out if h == 0 else jnp.where(mine, out, dq)
    dqkv = jnp.concatenate(
        [
            (dq * hd**-0.5).astype(bf16),
            (jnp.concatenate(dk, 0) * (1.0 / LOG2E)).astype(bf16).T,
            jnp.concatenate(dv, 0).astype(bf16).T,
        ],
        1,
    )
    gq[...] += dot(y, dqkv, 0, 0)
    d_shift = dot(dqkv, w_qkv[...], 1, 1).astype(bf16).astype(f32)
    return dx1 + layer_norm_backward(d_shift, g1, xhat1, rstd1)


def halves(tile):
    return tile.reshape(tile.shape[0] // 2, 2 * tile.shape[1], tile.shape[2]).astype(bf16)


def unhalves(packed):
    return packed.astype(f32).reshape(packed.shape[0] * 2, packed.shape[1] // 2, packed.shape[2])


def block_kernel(
    n_row, n_col, factor,
    frames, cotangent, gain1, w_qkv, rel_bias, w_proj, gain2, w_up, w_down,
    grad, g_qkv, g_proj, g_up, g_down,
    to_left, to_up, to_diag, from_right, from_down, from_diag,
    to_right, to_down, to_diag2, from_left, from_up, from_diag2,
    tile, probs, bias, gq, gp, gu, gd,
    red, red_send, red_core, red_x, red_z, red_y, full,
    in_send, in_recv, out_send, out_recv, grad_sem, red_ssem, red_rsem,
):
    nfr, tile_h, tile_w, chan = frames.shape
    row, col = lax.axis_index("row"), lax.axis_index("col")
    n_z = min(4, n_row)
    n_yh = n_row // n_z
    n_x = min(4, n_col // 2)
    n_yl = n_col // (2 * n_x)
    n_y = n_yh * n_yl
    core, x_at, y_lo = lax.rem(col, 2), lax.rem(col // 2, n_x), col // (2 * n_x)
    z_at, y_hi = lax.rem(row, n_z), row // n_z
    y_at = y_hi * n_yl + y_lo

    left, right = lax.rem(col + n_col - 1, n_col), lax.rem(col + 1, n_col)
    up, down = lax.rem(row + n_row - 1, n_row), lax.rem(row + 1, n_row)
    in_to = ((row, left), (up, col), (up, left))
    out_to = ((row, right), (down, col), (down, right))

    def core_peer(s):
        return (row, col + 1 - 2 * core)

    def x_peer(s):
        return (row, (y_lo * n_x + lax.rem(x_at + s, n_x)) * 2 + core)

    def z_peer(s):
        return (y_hi * n_z + lax.rem(z_at + s, n_z), col)

    def y_peer(s):
        other = lax.rem(y_at + s, n_y)
        return ((other // n_yl) * n_z + z_at, (lax.rem(other, n_yl) * n_x + x_at) * 2 + core)

    peers = list(in_to) + list(out_to) + [core_peer(1)]
    peers += [x_peer(s) for s in range(1, n_x)]
    peers += [z_peer(s) for s in range(1, n_z)]
    peers += [y_peer(s) for s in range(1, n_y)]
    barrier = pltpu.get_barrier_semaphore()
    for peer in peers:
        pl.semaphore_signal(barrier, inc=1, device_id=peer, device_id_type=MESH)
    pl.semaphore_wait(barrier, len(peers))

    def in_copies(f):
        pairs = ((to_left, from_right), (to_up, from_down), (to_diag, from_diag))
        return [
            pltpu.make_async_remote_copy(
                src_ref=a.at[f], dst_ref=b.at[f],
                send_sem=in_send.at[i, f], recv_sem=in_recv.at[i, f],
                device_id=in_to[i], device_id_type=MESH,
            )
            for i, (a, b) in enumerate(pairs)
        ]

    def out_copies(f):
        pairs = ((to_right, from_left), (to_down, from_up), (to_diag2, from_diag2))
        return [
            pltpu.make_async_remote_copy(
                src_ref=a.at[f], dst_ref=b.at[f],
                send_sem=out_send.at[i, f], recv_sem=out_recv.at[i, f],
                device_id=out_to[i], device_id_type=MESH,
            )
            for i, (a, b) in enumerate(pairs)
        ]

    def send_in(f):
        for i, source in enumerate((frames, cotangent)):
            whole = source[f].astype(f32)
            to_left[f, i] = halves(whole[SHIFT:, :SHIFT])
            to_up[f, i] = halves(whole[:SHIFT, SHIFT:])
            to_diag[f, i] = halves(whole[:SHIFT, :SHIFT])
        for copy in in_copies(f):
            copy.start()

    def grad_copy(f):
        return pltpu.make_async_copy(tile.at[f], grad.at[f], grad_sem.at[f])

    def finish(f):
        for copy in out_copies(f):
            copy.wait_recv()
        tile[f, SHIFT:, :SHIFT] = unhalves(from_left[f])
        tile[f, :SHIFT, SHIFT:] = unhalves(from_up[f])
        tile[f, :SHIFT, :SHIFT] = unhalves(from_diag2[f])
        grad_copy(f).start()

    ahead = min(3, nfr)
    for f in range(ahead):
        send_in(f)

    wide = WS * WS
    at_q = lax.broadcasted_iota(jnp.int32, (wide, wide), 0)
    at_k = lax.broadcasted_iota(jnp.int32, (wide, wide), 1)
    cut_row = (at_q // (WS * SHIFT)) != (at_k // (WS * SHIFT))
    cut_col = (lax.rem(at_q, WS) // SHIFT) != (lax.rem(at_k, WS) // SHIFT)
    last_row = jnp.where(row == n_row - 1, 1.0, 0.0)
    last_col = jnp.where(col == n_col - 1, 1.0, 0.0)
    by_row = jnp.where(cut_row, last_row, 0.0)
    by_col = jnp.where(cut_col, last_col, 0.0)
    windows = tile_h // WS
    for w in range(windows):
        cut = jnp.maximum(by_row, by_col) if w == windows - 1 else by_col
        for h in range(HEADS):
            bias[w, h] = (rel_bias[h] + cut * -100.0) * LOG2E
    for ref in (gq, gp, gu, gd):
        ref[...] = jnp.zeros_like(ref)

    def frame_step(f, carry):
        @pl.when(f + ahead < nfr)
        def _():
            send_in(f + ahead)

        for copy in in_copies(f):
            copy.wait_recv()
        parts = []
        for i, source in enumerate((frames, cotangent)):
            own = source[f].astype(f32)[SHIFT:, SHIFT:]
            first = jnp.concatenate([own, unhalves(from_down[f, i])], 0)
            second = jnp.concatenate([unhalves(from_right[f, i]), unhalves(from_diag[f, i])], 0)
            shifted = jnp.concatenate([first, second], 1)
            parts.append(
                [shifted[w * WS : (w + 1) * WS].reshape(wide, chan) for w in range(windows)]
            )
        result = []
        for w in range(windows):
            out = window_block(
                parts[0][w], parts[1][w], w, gain1[...], gain2[...], w_qkv, w_proj, w_up, w_down,
                bias, probs, (gq, gp, gu, gd),
            )
            result.append(out.reshape(WS, WS, chan))
        out = jnp.concatenate(result, 0)
        keep = tile_h - SHIFT
        to_right[f] = halves(out[:keep, SHIFT:])
        to_down[f] = halves(out[keep:, :SHIFT])
        to_diag2[f] = halves(out[keep:, SHIFT:])
        for copy in out_copies(f):
            copy.start()
        tile[f, SHIFT:, SHIFT:] = out[:keep, :SHIFT]

        @pl.when(f >= 2)
        def _():
            finish(f - 2)

        return carry

    lax.fori_loop(0, nfr, frame_step, 0)

    for j in range(3):
        red[chan * j : chan * (j + 1)] = gq[:, chan * j : chan * (j + 1)]
    red[3 * chan : 4 * chan] = gp[...]
    for j in range(4):
        red[chan * (4 + j) : chan * (5 + j)] = gu[:, chan * j : chan * (j + 1)]
        red[chan * (8 + j) : chan * (9 + j)] = gd[:, chan * j : chan * (j + 1)]
    rows = red.shape[0]
    size_c = rows // 2
    size_x = size_c // n_x
    size_z = size_x // n_z

    def copy_to(peer, src, dst, sem):
        return pltpu.make_async_remote_copy(
            src_ref=src, dst_ref=dst, send_sem=red_ssem.at[sem], recv_sem=red_rsem.at[sem],
            device_id=peer, device_id_type=MESH,
        )

    def at(start, size):
        return pl.ds(pl.multiple_of(start, 16), size)

    red_send[...] = red[...].astype(bf16)
    sem = 0
    copies = []
    base = core * size_c
    first = copy_to(core_peer(1), red_send.at[at((1 - core) * size_c, size_c)], red_core, sem)
    first.start()
    copies.append(first)
    sem += 1
    for f in range(max(nfr - 2, 0), nfr):
        finish(f)
    first.wait_recv()
    red[at(base, size_c)] += red_core[...].astype(f32)

    def reduce_stage(base, size, n, index, peer, landing, sem):
        red_send2 = red_stage[len(landings)]
        landings.append(0)
        red_send2[...] = red[at(base, size * n)].astype(bf16)
        started = []
        for s in range(1, n):
            other = lax.rem(index + s, n)
            started.append(
                copy_to(peer(s), red_send2.at[at(other * size, size)], landing.at[s - 1], sem)
            )
            started[-1].start()
            sem += 1
        base = base + index * size
        for copy in started:
            copy.wait_recv()
        total = red[at(base, size)]
        for s in range(1, n):
            total += landing[s - 1].astype(f32)
        red[at(base, size)] = total
        copies.extend(started)
        return base, sem

    landings = []
    red_stage = (full.at[pl.ds(rows, size_c)], full.at[pl.ds(rows + size_c, size_x)])
    base, sem = reduce_stage(base, size_x, n_x, x_at, x_peer, red_x, sem)
    base, sem = reduce_stage(base, size_z, n_z, z_at, z_peer, red_z, sem)
    red_y[y_at] = red[at(base, size_z)].astype(bf16)
    started = []
    for s in range(1, n_y):
        started.append(copy_to(y_peer(s), red_y.at[y_at], red_y.at[y_at], sem))
        started[-1].start()
        sem += 1
    for copy in started:
        copy.wait_recv()
    copies.extend(started)
    total = red_y[0].astype(f32)
    for j in range(1, n_y):
        total += red_y[j].astype(f32)
    full[at(base, size_z)] = total.astype(bf16)

    def gather_stage(base, size, n, peer, sem):
        started = []
        for s in range(1, n):
            part = full.at[at(base, size)]
            started.append(copy_to(peer(s), part, part, sem))
            started[-1].start()
            sem += 1
        for copy in started:
            copy.wait_recv()
        copies.extend(started)
        return sem

    sem = gather_stage(base, size_z, n_z, z_peer, sem)
    sem = gather_stage(core * size_c + x_at * size_x, size_x, n_x, x_peer, sem)
    sem = gather_stage(core * size_c, size_c, 2, core_peer, sem)
    for j in range(3):
        g_qkv[:, chan * j : chan * (j + 1)] = (
            full[chan * j : chan * (j + 1)].astype(f32) * factor
        )
    g_proj[...] = full[3 * chan : 4 * chan].astype(f32) * factor
    for j in range(4):
        g_up[:, chan * j : chan * (j + 1)] = (
            full[chan * (4 + j) : chan * (5 + j)].astype(f32) * factor
        )
        g_down[chan * j : chan * (j + 1)] = (
            full[chan * (8 + j) : chan * (9 + j)].astype(f32) * factor
        ).T
    for copy in copies:
        copy.wait_send()

    def drain(f, carry):
        for copy in in_copies(f) + out_copies(f):
            copy.wait_send()
        grad_copy(f).wait()
        return carry

    lax.fori_loop(0, nfr, drain, 0)


def solution(mesh):
    n_row, n_col = mesh.shape["row"], mesh.shape["col"]

    def shards(frames, cotangent, gain1, w_qkv, rel_bias, w_proj, gain2, w_up, w_down):
        nfr, tile_h, tile_w, chan = frames.shape
        ff = w_up.shape[1]
        factor = float(nfr * tile_h * tile_w * n_row * n_col) ** -0.5
        long, short = (tile_h - SHIFT) // 2, SHIFT // 2
        wide = WS * WS
        rows = 4 * chan + 2 * ff
        n_z, n_x = min(4, n_row), min(4, n_col // 2)
        n_y = (n_row // n_z) * (n_col // (2 * n_x))
        size_c = rows // 2
        size_x = size_c // n_x
        size_z = size_x // n_z
        n_sem = 2 + 2 * (n_x - 1) + 2 * (n_z - 1) + (n_y - 1)

        def pieces(k):
            sizes = (long, short, short)
            lead = (nfr,) if k == 1 else (nfr, k)
            return [pltpu.VMEM(lead + (s, 2 * SHIFT, chan), bf16) for s in sizes]

        vmem = pl.BlockSpec(memory_space=pltpu.VMEM)
        return pl.pallas_call(
            functools.partial(block_kernel, n_row, n_col, factor),
            out_shape=[
                jax.ShapeDtypeStruct(frames.shape, f32),
                jax.ShapeDtypeStruct((chan, 3 * chan), f32),
                jax.ShapeDtypeStruct((chan, chan), f32),
                jax.ShapeDtypeStruct((chan, ff), f32),
                jax.ShapeDtypeStruct((ff, chan), f32),
            ],
            in_specs=[vmem] * 9,
            out_specs=[pl.BlockSpec(memory_space=pl.ANY)] + [vmem] * 4,
            scratch_shapes=pieces(2) + pieces(2) + pieces(1) + pieces(1)
            + [
                pltpu.VMEM(frames.shape, f32),
                pltpu.VMEM((tile_h // WS, HEADS, wide, wide), bf16),
                pltpu.VMEM((tile_h // WS, HEADS, wide, wide), f32),
                pltpu.VMEM((chan, 3 * chan), f32),
                pltpu.VMEM((chan, chan), f32),
                pltpu.VMEM((chan, ff), f32),
                pltpu.VMEM((chan, ff), f32),
                pltpu.VMEM((rows, chan), f32),
                pltpu.VMEM((rows, chan), bf16),
                pltpu.VMEM((size_c, chan), bf16),
                pltpu.VMEM((max(n_x - 1, 1), size_x, chan), bf16),
                pltpu.VMEM((max(n_z - 1, 1), size_z, chan), bf16),
                pltpu.VMEM((n_y, size_z, chan), bf16),
                pltpu.VMEM((rows + size_c + size_x, chan), bf16),
                pltpu.SemaphoreType.DMA((3, nfr)),
                pltpu.SemaphoreType.DMA((3, nfr)),
                pltpu.SemaphoreType.DMA((3, nfr)),
                pltpu.SemaphoreType.DMA((3, nfr)),
                pltpu.SemaphoreType.DMA((nfr,)),
                pltpu.SemaphoreType.DMA((n_sem,)),
                pltpu.SemaphoreType.DMA((n_sem,)),
            ],
            compiler_params=pltpu.CompilerParams(
                collective_id=0, has_side_effects=True, vmem_limit_bytes=56 * 2**20
            ),
        )(
            frames, cotangent, gain1.reshape(1, chan), w_qkv, rel_bias, w_proj,
            gain2.reshape(1, chan), w_up, w_down,
        )

    tiles = P(None, "row", "col", None)
    return jax.shard_map(
        shards,
        mesh=mesh,
        in_specs=(tiles, tiles) + (P(),) * 7,
        out_specs=(tiles, P(), P(), P(), P()),
        check_vma=False,
    )
```

time: 645 us -> 166 us (0.26)
  matrix products: 257 us -> 0 us
  waiting for transfers between devices: 219 us -> 0 us
  Pallas kernels: 0 us -> 158 us
  other arithmetic: 68.2 us -> 0 us
  local copies, waits for them, and re-layouts: 58.8 us -> 7.39 us
  starting transfers between devices: 21.3 us -> 0 us
  between operations: 15 us -> 0.68 us
    dot_general x31 -> x0, matrix products: 193 us -> none  [the longest x4 51.9 us: attend_bwd(): jnp.einsum('bhlm,bmhd->blhd', d_score, keys, preferred_element_type=jnp.f...]
    pallas_call x0 -> x1, Pallas kernels: none -> 158 us  [shards(): pl.pallas_call(functools.partial(block_kernel, n_row, n_col, factor), out...]
    psum x1 -> x0, waiting for transfers between devices: 148 us -> none  [shards(): lax.psum((g_down, g_up, g_proj, g_qkv), ('row', 'col'))]
    ppermute x8 -> x0, waiting for transfers between devices: 70.5 us -> none  [from_behind(): return lax.ppermute(block, axis, route)]
    sub x8 -> x0, matrix products: 63.4 us -> none  [probabilities(): scores = scores - jnp.max(scores, -1, keepdims=True)]
    reduce_sum x6 -> x0, other arithmetic: 23.9 us -> none  [the longest x1 6.86 us: layer_norm_backward(): jnp.mean(normalized_gradient * normalized_input, -1, keepdims=True)]
    ppermute x8 -> x0, starting transfers between devices: 21.3 us -> none  [from_behind(): return lax.ppermute(block, axis, route)]
    dynamic_update_slice x16 -> x0, local copies, waits for them, and re-layouts: 13.3 us -> none  [blocked(): result = lax.map(lambda items: func(*items), grouped)]
  transfers between devices with their start and end apart: 9 -> 0, of which waited for: 8 -> 0; matrix products, arithmetic and copies ran while one was open for 4% -> 0% of each run, Pallas kernels for 0% -> 0%
where the time goes in v1:
time: 166 us
  Pallas kernels  158 us (95%)
  local copies, waits for them, and re-layouts  7.39 us (4%)
    pallas_call x1, Pallas kernels, shards(): pl.pallas_call(functools.partial(block_kernel, n_row, n_col, factor), out...  158 us
    unnamed x13, local copies, waits for them, and re-layouts  7.39 us

profile of v1, /device:TPU:1, one launch (start us, length us, event | category | flops | bytes accessed | tf_op | source)
XLA Modules:
  0.0 166.0 jit_solution(4240321208976926661)
XLA Ops:
  0.6 158.0 %shard_map.128 = (f32[16,32,16,128]{3,2,1,0:T(8,128)}, f32[128,384]{1,0:T(8,128)}, f32[128,128]{1,0:T(8,128)}, f32[128,512]{1,0:T(8,128)}, f32[512,128]{1,0:T(8,128)}) custom-call(bf16[16,32,16,128]{3,2,1,0:T(8,128)(2,1)} %frames.1, bf16[16,32,16,128]{3,2,1,0:T(8,128)(2,1)} %cotangent.1, f32[1,128]{1,0:T(1,128)} %bitcast.2, bf16[128,384]{1,0:T(8,128)(2,1)} %w_qkv.1, ...), custom_call_target="tpu_custom_call" | custom-call | tf_op jit(solution)/shard_map/pallas_call | solution.py:410
  158.6 0.0 copy-start.2
  158.6 0.0 copy-start.3
  158.6 0.0 copy-start.1
  158.6 0.0 copy-start
  158.6 4.7 %copy.19 = f32[16,32,16,128]{3,2,1,0:T(8,128)} copy(f32[16,32,16,128]{3,2,1,0:T(8,128)} %get-tuple-element.10) | data formatting | bytes 8388608
  163.3 0.0 copy-done.2
  163.3 0.7 copy.20
  164.0 0.0 copy-done.3
  164.0 0.6 copy.21
  164.6 0.0 copy-done.1
  164.6 0.7 copy.22
  165.3 0.0 copy-done
  165.3 0.7 copy.23
Async XLA Ops:
  158.6 4.7 %copy-start.2 = (f32[128,384]{1,0:T(8,128)S(1)}, f32[128,384]{1,0:T(8,128)}, u32[]{:S(2)}) copy-start(f32[128,384]{1,0:T(8,128)} %get-tuple-element.11) | copy-start | bytes 589828
  158.6 5.4 %copy-start.3 = (f32[128,128]{1,0:T(8,128)S(1)}, f32[128,128]{1,0:T(8,128)}, u32[]{:S(2)}) copy-start(f32[128,128]{1,0:T(8,128)} %get-tuple-element.12) | copy-start | bytes 196612
  158.6 6.0 %copy-start.1 = (f32[128,512]{1,0:T(8,128)S(1)}, f32[128,512]{1,0:T(8,128)}, u32[]{:S(2)}) copy-start(f32[128,512]{1,0:T(8,128)} %get-tuple-element.13) | copy-start | bytes 786436
  158.6 6.7 %copy-start = (f32[512,128]{1,0:T(8,128)S(1)}, f32[512,128]{1,0:T(8,128)}, u32[]{:S(2)}) copy-start(f32[512,128]{1,0:T(8,128)} %get-tuple-element.14) | copy-start | bytes 786436

commit v2 on v1

--- a/solution.py
+++ b/solution.py
@@ -16,6 +16,7 @@
 MESH = pl.DeviceIdType.MESH
 bf16 = jnp.bfloat16
 f32 = jnp.float32
+PER = 2
 
 
 def dot(a, b, ca, cb):
@@ -48,58 +49,85 @@
     return u * cdf, cdf + u * expo * (1.0 / math.sqrt(2.0 * math.pi))
 
 
-def window_block(x, c, w, g1, g2, w_qkv, w_proj, w_up, w_down, bias, probs, acc):
+def window_block(at, x, c, bias, g1, g2, w_qkv, w_proj, w_up, w_down, probs, acc, result):
     gq, gp, gu, gd = acc
     tokens, chan = x.shape
     hd = chan // HEADS
+    ff = w_up.shape[1]
     head = lax.broadcasted_iota(jnp.int32, (tokens, chan), 1) // hd
     xhat1, rstd1 = layer_norm_stats(x)
     y = (xhat1 * g1).astype(bf16)
+    yield
     qkv = dot(y, w_qkv[...], 1, 0)
+    yield
     q = qkv[:, :chan] * (LOG2E / math.sqrt(hd))
     k = qkv[:, chan : 2 * chan].astype(bf16)
     v_one = jnp.concatenate([qkv[:, 2 * chan :].astype(bf16), jnp.ones((tokens, chan), bf16)], 1)
+    yield
     total, norm = None, None
     for h in range(HEADS):
         mine = head == h
-        scores = dot(jnp.where(mine, q, 0.0).astype(bf16), k, 1, 1) + bias[w, h]
+        scores = dot(jnp.where(mine, q, 0.0).astype(bf16), k, 1, 1) + bias[h]
+        yield
         expo = jnp.exp2(scores - jnp.max(scores, -1, keepdims=True)).astype(bf16)
-        probs[w, h] = expo
+        probs[at, h] = expo
+        yield
         out = dot(expo, v_one, 1, 0)
         total = out[:, :chan] if h == 0 else jnp.where(mine, out[:, :chan], total)
         norm = out[:, chan:] if h == 0 else jnp.where(mine, out[:, chan:], norm)
+        yield
     inverse = 1.0 / norm
     attended = total * inverse
     attended_b = attended.astype(bf16)
     proj = dot(attended_b, w_proj[...], 1, 0).astype(bf16)
+    yield
     x1 = (x + proj.astype(f32)).astype(bf16).astype(f32)
     xhat2, rstd2 = layer_norm_stats(x1)
     z = (xhat2 * g2).astype(bf16)
     c_b = c.astype(bf16)
-    act, slope = gelu_and_slope(dot(z, w_up[...], 1, 0))
-    hid = act.astype(bf16)
-    du = (dot(c_b, w_down[...], 1, 1) * slope).astype(bf16)
-    gd[...] += dot(c_b, hid, 0, 0)
-    gu[...] += dot(z, du, 0, 0)
-    dx1 = c + layer_norm_backward(dot(du, w_up[...], 1, 1), g2, xhat2, rstd2)
+    yield
+    z_t, c_t = z.T, c_b.T
+    dz = None
+    part = ff // 2
+    for j in range(0, ff, part):
+        u = dot(z, w_up[:, j : j + part], 1, 0)
+        d_hid = dot(c_b, w_down[j : j + part, :], 1, 1)
+        yield
+        act, slope = gelu_and_slope(u)
+        hid = act.astype(bf16)
+        du = (d_hid * slope).astype(bf16)
+        yield
+        gd[:, j : j + part] += dot(c_t, hid, 1, 0)
+        gu[:, j : j + part] += dot(z_t, du, 1, 0)
+        more = dot(du, w_up[:, j : j + part], 1, 1)
+        dz = more if dz is None else dz + more
+        yield
+    dx1 = c + layer_norm_backward(dz, g2, xhat2, rstd2)
     dx1_b = dx1.astype(bf16)
     gp[...] += dot(attended_b, dx1_b, 0, 0)
-    d_att = dot(dx1_b, w_proj[...], 1, 1).astype(bf16).astype(f32) * inverse
+    d_att = dot(dx1_b, w_proj[...], 1, 1).astype(bf16).astype(f32)
+    yield
+    d_att = d_att * inverse
     d_sum = -(d_att * attended)
     q_t = q.astype(bf16).T
     d_att_t = d_att.astype(bf16).T
+    yield
     dv, dk, dq = [], [], None
     for h in range(HEADS):
         mine = head == h
         left = jnp.concatenate(
             [jnp.where(mine, d_att, 0.0).astype(bf16), jnp.where(mine, d_sum, 0.0).astype(bf16)], 1
         )
-        expo = probs[w, h]
-        ds = (expo.astype(f32) * dot(left, v_one, 1, 1)).astype(bf16)
+        d_prob = dot(left, v_one, 1, 1)
+        yield
+        expo = probs[at, h]
+        ds = (expo.astype(f32) * d_prob).astype(bf16)
+        yield
         dv.append(dot(d_att_t[hd * h : hd * (h + 1)], expo, 1, 0))
         dk.append(dot(q_t[hd * h : hd * (h + 1)], ds, 1, 0))
         out = dot(ds, k, 1, 0)
         dq = out if h == 0 else jnp.where(mine, out, dq)
+        yield
     dqkv = jnp.concatenate(
         [
             (dq * hd**-0.5).astype(bf16),
@@ -108,9 +136,16 @@
         ],
         1,
     )
+    yield
     gq[...] += dot(y, dqkv, 0, 0)
     d_shift = dot(dqkv, w_qkv[...], 1, 1).astype(bf16).astype(f32)
-    return dx1 + layer_norm_backward(d_shift, g1, xhat1, rstd1)
+    result[at] = dx1 + layer_norm_backward(d_shift, g1, xhat1, rstd1)
+    yield
+
+
+def take_turns(stages):
+    while stages:
+        stages = [one for one in stages if next(one, stages) is not stages]
 
 
 def halves(tile):
@@ -122,17 +157,36 @@
 
 
 def block_kernel(
-    n_row, n_col, factor,
-    frames, cotangent, gain1, w_qkv, rel_bias, w_proj, gain2, w_up, w_down,
-    grad, g_qkv, g_proj, g_up, g_down,
+    n_row, n_col,
+    frames_in, cotangent_in, gain1, w_qkv, bias_in, w_proj, gain2, w_up, w_down,
+    grad, full_out,
+    frames, cotangent, rel_bias,
     to_left, to_up, to_diag, from_right, from_down, from_diag,
     to_right, to_down, to_diag2, from_left, from_up, from_diag2,
-    tile, probs, bias, gq, gp, gu, gd,
+    own_out, tile, probs, bias, gq, gp, gu, gd,
     red, red_send, red_core, red_x, red_z, red_y, full,
-    in_send, in_recv, out_send, out_recv, grad_sem, red_ssem, red_rsem,
+    load_sem, in_send, in_recv, out_send, out_recv, grad_sem, red_ssem, red_rsem,
 ):
     nfr, tile_h, tile_w, chan = frames.shape
+    steps = nfr // PER
     row, col = lax.axis_index("row"), lax.axis_index("col")
+
+    def loads(s):
+        span = pl.ds(s * PER, PER)
+        return [
+            pltpu.make_async_copy(frames_in.at[span], frames.at[span], load_sem.at[0, s]),
+            pltpu.make_async_copy(cotangent_in.at[span], cotangent.at[span], load_sem.at[1, s]),
+        ]
+
+    bias_load = pltpu.make_async_copy(bias_in, rel_bias, load_sem.at[0, steps])
+    for s in range(min(2, steps)):
+        for copy in loads(s):
+            copy.start()
+    bias_load.start()
+    for s in range(2, steps):
+        for copy in loads(s):
+            copy.start()
+
     n_z = min(4, n_row)
     n_yh = n_row // n_z
     n_x = min(4, n_col // 2)
@@ -169,52 +223,63 @@
         pl.semaphore_signal(barrier, inc=1, device_id=peer, device_id_type=MESH)
     pl.semaphore_wait(barrier, len(peers))
 
-    def in_copies(f):
+    def in_copies(s):
+        span = pl.ds(s * PER, PER)
         pairs = ((to_left, from_right), (to_up, from_down), (to_diag, from_diag))
         return [
             pltpu.make_async_remote_copy(
-                src_ref=a.at[f], dst_ref=b.at[f],
-                send_sem=in_send.at[i, f], recv_sem=in_recv.at[i, f],
+                src_ref=a.at[span], dst_ref=b.at[span],
+                send_sem=in_send.at[i, s], recv_sem=in_recv.at[i, s],
                 device_id=in_to[i], device_id_type=MESH,
             )
             for i, (a, b) in enumerate(pairs)
         ]
 
-    def out_copies(f):
+    def out_copies(s):
+        span = pl.ds(s * PER, PER)
         pairs = ((to_right, from_left), (to_down, from_up), (to_diag2, from_diag2))
         return [
             pltpu.make_async_remote_copy(
-                src_ref=a.at[f], dst_ref=b.at[f],
-                send_sem=out_send.at[i, f], recv_sem=out_recv.at[i, f],
+                src_ref=a.at[span], dst_ref=b.at[span],
+                send_sem=out_send.at[i, s], recv_sem=out_recv.at[i, s],
                 device_id=out_to[i], device_id_type=MESH,
             )
             for i, (a, b) in enumerate(pairs)
         ]
 
-    def send_in(f):
-        for i, source in enumerate((frames, cotangent)):
-            whole = source[f].astype(f32)
-            to_left[f, i] = halves(whole[SHIFT:, :SHIFT])
-            to_up[f, i] = halves(whole[:SHIFT, SHIFT:])
-            to_diag[f, i] = halves(whole[:SHIFT, :SHIFT])
-        for copy in in_copies(f):
+    def send_in(s):
+        for copy in loads(s):
+            copy.wait()
+        for f in range(PER):
+            at = s * PER + f
+            for i, source in enumerate((frames, cotangent)):
+                whole = source[at].astype(f32)
+                to_left[at, i] = halves(whole[SHIFT:, :SHIFT])
+                to_up[at, i] = halves(whole[:SHIFT, SHIFT:])
+                to_diag[at, i] = halves(whole[:SHIFT, :SHIFT])
+        for copy in in_copies(s):
             copy.start()
 
-    def grad_copy(f):
-        return pltpu.make_async_copy(tile.at[f], grad.at[f], grad_sem.at[f])
-
-    def finish(f):
-        for copy in out_copies(f):
+    def grad_copy(s):
+        span = pl.ds(s * PER, PER)
+        return pltpu.make_async_copy(tile.at[span], grad.at[span], grad_sem.at[s])
+
+    def finish(s):
+        for copy in out_copies(s):
             copy.wait_recv()
-        tile[f, SHIFT:, :SHIFT] = unhalves(from_left[f])
-        tile[f, :SHIFT, SHIFT:] = unhalves(from_up[f])
-        tile[f, :SHIFT, :SHIFT] = unhalves(from_diag2[f])
-        grad_copy(f).start()
-
-    ahead = min(3, nfr)
-    for f in range(ahead):
-        send_in(f)
-
+        for f in range(PER):
+            at = s * PER + f
+            top = jnp.concatenate([unhalves(from_diag2[at]), unhalves(from_up[at])], 1)
+            tile[at, :SHIFT] = top.astype(bf16)
+            rest = jnp.concatenate([unhalves(from_left[at]), unhalves(own_out[at])], 1)
+            tile[at, SHIFT:] = rest.astype(bf16)
+        grad_copy(s).start()
+
+    ahead = min(2, steps)
+    for s in range(ahead):
+        send_in(s)
+
+    bias_load.wait()
     wide = WS * WS
     at_q = lax.broadcasted_iota(jnp.int32, (wide, wide), 0)
     at_k = lax.broadcasted_iota(jnp.int32, (wide, wide), 1)
@@ -232,45 +297,52 @@
     for ref in (gq, gp, gu, gd):
         ref[...] = jnp.zeros_like(ref)
 
-    def frame_step(f, carry):
-        @pl.when(f + ahead < nfr)
+    def step(s, carry):
+        @pl.when(s + ahead < steps)
         def _():
-            send_in(f + ahead)
-
-        for copy in in_copies(f):
+            send_in(s + ahead)
+
+        for copy in in_copies(s):
             copy.wait_recv()
-        parts = []
-        for i, source in enumerate((frames, cotangent)):
-            own = source[f].astype(f32)[SHIFT:, SHIFT:]
-            first = jnp.concatenate([own, unhalves(from_down[f, i])], 0)
-            second = jnp.concatenate([unhalves(from_right[f, i]), unhalves(from_diag[f, i])], 0)
-            shifted = jnp.concatenate([first, second], 1)
-            parts.append(
-                [shifted[w * WS : (w + 1) * WS].reshape(wide, chan) for w in range(windows)]
-            )
-        result = []
-        for w in range(windows):
-            out = window_block(
-                parts[0][w], parts[1][w], w, gain1[...], gain2[...], w_qkv, w_proj, w_up, w_down,
-                bias, probs, (gq, gp, gu, gd),
-            )
-            result.append(out.reshape(WS, WS, chan))
-        out = jnp.concatenate(result, 0)
+        stages, result = [], [None] * (PER * windows)
+        for f in range(PER):
+            at = s * PER + f
+            parts = []
+            for i, source in enumerate((frames, cotangent)):
+                own = source[at].astype(f32)[SHIFT:, SHIFT:]
+                first = jnp.concatenate([own, unhalves(from_down[at, i])], 0)
+                second = jnp.concatenate(
+                    [unhalves(from_right[at, i]), unhalves(from_diag[at, i])], 0
+                )
+                parts.append(jnp.concatenate([first, second], 1))
+            for w in range(windows):
+                x, c = (p[w * WS : (w + 1) * WS].reshape(wide, chan) for p in parts)
+                stages.append(
+                    window_block(
+                        f * windows + w, x, c, bias.at[w], gain1[...], gain2[...],
+                        w_qkv, w_proj, w_up, w_down, probs, (gq, gp, gu, gd), result,
+                    )
+                )
+        take_turns(stages)
         keep = tile_h - SHIFT
-        to_right[f] = halves(out[:keep, SHIFT:])
-        to_down[f] = halves(out[keep:, :SHIFT])
-        to_diag2[f] = halves(out[keep:, SHIFT:])
-        for copy in out_copies(f):
+        for f in range(PER):
+            at = s * PER + f
+            out = [r.reshape(WS, WS, chan) for r in result[f * windows : (f + 1) * windows]]
+            out = jnp.concatenate(out, 0)
+            to_right[at] = halves(out[:keep, SHIFT:])
+            to_down[at] = halves(out[keep:, :SHIFT])
+            to_diag2[at] = halves(out[keep:, SHIFT:])
+            own_out[at] = halves(out[:keep, :SHIFT])
+        for copy in out_copies(s):
             copy.start()
-        tile[f, SHIFT:, SHIFT:] = out[:keep, :SHIFT]
-
-        @pl.when(f >= 2)
+
+        @pl.when(s >= 1)
         def _():
-            finish(f - 2)
+            finish(s - 1)
 
         return carry
 
-    lax.fori_loop(0, nfr, frame_step, 0)
+    lax.fori_loop(0, steps, step, 0)
 
     for j in range(3):
         red[chan * j : chan * (j + 1)] = gq[:, chan * j : chan * (j + 1)]
@@ -300,8 +372,7 @@
     first.start()
     copies.append(first)
     sem += 1
-    for f in range(max(nfr - 2, 0), nfr):
-        finish(f)
+    finish(steps - 1)
     first.wait_recv()
     red[at(base, size_c)] += red_core[...].astype(f32)
 
@@ -360,28 +431,35 @@
     sem = gather_stage(base, size_z, n_z, z_peer, sem)
     sem = gather_stage(core * size_c + x_at * size_x, size_x, n_x, x_peer, sem)
     sem = gather_stage(core * size_c, size_c, 2, core_peer, sem)
-    for j in range(3):
-        g_qkv[:, chan * j : chan * (j + 1)] = (
-            full[chan * j : chan * (j + 1)].astype(f32) * factor
-        )
-    g_proj[...] = full[3 * chan : 4 * chan].astype(f32) * factor
-    for j in range(4):
-        g_up[:, chan * j : chan * (j + 1)] = (
-            full[chan * (4 + j) : chan * (5 + j)].astype(f32) * factor
-        )
-        g_down[chan * j : chan * (j + 1)] = (
-            full[chan * (8 + j) : chan * (9 + j)].astype(f32) * factor
-        ).T
+    full_out[...] = full[:rows]
     for copy in copies:
         copy.wait_send()
 
-    def drain(f, carry):
-        for copy in in_copies(f) + out_copies(f):
+    def drain(s, carry):
+        for copy in in_copies(s) + out_copies(s):
             copy.wait_send()
-        grad_copy(f).wait()
+        grad_copy(s).wait()
         return carry
 
-    lax.fori_loop(0, nfr, drain, 0)
+    lax.fori_loop(0, steps, drain, 0)
+
+
+def finish_kernel(factor, grad_b, full, grad, g_qkv, g_proj, g_up, g_down):
+    grad[...] = grad_b[...].astype(f32)
+
+    @pl.when(pl.program_id(0) == 0)
+    def _():
+        chan = full.shape[1]
+
+        def block(j):
+            return full[chan * j : chan * (j + 1)].astype(f32) * factor
+
+        for j in range(g_qkv.shape[1] // chan):
+            g_qkv[:, chan * j : chan * (j + 1)] = block(j)
+        g_proj[...] = block(3)
+        for j in range(g_up.shape[1] // chan):
+            g_up[:, chan * j : chan * (j + 1)] = block(4 + j)
+            g_down[chan * j : chan * (j + 1)] = block(8 + j).T
 
 
 def solution(mesh):
@@ -404,25 +482,30 @@
         def pieces(k):
             sizes = (long, short, short)
             lead = (nfr,) if k == 1 else (nfr, k)
-            return [pltpu.VMEM(lead + (s, 2 * SHIFT, chan), bf16) for s in sizes]
+            return [pltpu.VMEM(lead + (n, 2 * SHIFT, chan), bf16) for n in sizes]
 
         vmem = pl.BlockSpec(memory_space=pltpu.VMEM)
-        return pl.pallas_call(
-            functools.partial(block_kernel, n_row, n_col, factor),
+        hbm = pl.BlockSpec(memory_space=pl.ANY)
+        steps, windows = nfr // PER, tile_h // WS
+        grad_b, full = pl.pallas_call(
+            functools.partial(block_kernel, n_row, n_col),
             out_shape=[
-                jax.ShapeDtypeStruct(frames.shape, f32),
-                jax.ShapeDtypeStruct((chan, 3 * chan), f32),
-                jax.ShapeDtypeStruct((chan, chan), f32),
-                jax.ShapeDtypeStruct((chan, ff), f32),
-                jax.ShapeDtypeStruct((ff, chan), f32),
+                jax.ShapeDtypeStruct(frames.shape, bf16),
+                jax.ShapeDtypeStruct((rows, chan), bf16),
             ],
-            in_specs=[vmem] * 9,
-            out_specs=[pl.BlockSpec(memory_space=pl.ANY)] + [vmem] * 4,
-            scratch_shapes=pieces(2) + pieces(2) + pieces(1) + pieces(1)
+            in_specs=[hbm, hbm, vmem, vmem, hbm, vmem, vmem, vmem, vmem],
+            out_specs=[hbm, vmem],
+            scratch_shapes=[
+                pltpu.VMEM(frames.shape, bf16),
+                pltpu.VMEM(frames.shape, bf16),
+                pltpu.VMEM(rel_bias.shape, f32),
+            ]
+            + pieces(2) + pieces(2) + pieces(1) + pieces(1)
             + [
-                pltpu.VMEM(frames.shape, f32),
-                pltpu.VMEM((tile_h // WS, HEADS, wide, wide), bf16),
-                pltpu.VMEM((tile_h // WS, HEADS, wide, wide), f32),
+                pltpu.VMEM((nfr, long, 2 * SHIFT, chan), bf16),
+                pltpu.VMEM(frames.shape, bf16),
+                pltpu.VMEM((PER * windows, HEADS, wide, wide), bf16),
+                pltpu.VMEM((windows, HEADS, wide, wide), f32),
                 pltpu.VMEM((chan, 3 * chan), f32),
                 pltpu.VMEM((chan, chan), f32),
                 pltpu.VMEM((chan, ff), f32),
@@ -434,11 +517,12 @@
                 pltpu.VMEM((max(n_z - 1, 1), size_z, chan), bf16),
                 pltpu.VMEM((n_y, size_z, chan), bf16),
                 pltpu.VMEM((rows + size_c + size_x, chan), bf16),
-                pltpu.SemaphoreType.DMA((3, nfr)),
-                pltpu.SemaphoreType.DMA((3, nfr)),
-                pltpu.SemaphoreType.DMA((3, nfr)),
-                pltpu.SemaphoreType.DMA((3, nfr)),
-                pltpu.SemaphoreType.DMA((nfr,)),
+                pltpu.SemaphoreType.DMA((2, steps + 1)),
+                pltpu.SemaphoreType.DMA((3, steps)),
+                pltpu.SemaphoreType.DMA((3, steps)),
+                pltpu.SemaphoreType.DMA((3, steps)),
+                pltpu.SemaphoreType.DMA((3, steps)),
+                pltpu.SemaphoreType.DMA((steps,)),
                 pltpu.SemaphoreType.DMA((n_sem,)),
                 pltpu.SemaphoreType.DMA((n_sem,)),
             ],
@@ -450,6 +534,21 @@
             gain2.reshape(1, chan), w_up, w_down,
         )
 
+        def whole(shape):
+            return pl.BlockSpec(shape, lambda i: (0, 0))
+
+        chunk = pl.BlockSpec((PER,) + frames.shape[1:], lambda i: (i, 0, 0, 0))
+        sizes = [(chan, 3 * chan), (chan, chan), (chan, ff), (ff, chan)]
+        return pl.pallas_call(
+            functools.partial(finish_kernel, factor),
+            grid=(steps,),
+            out_shape=[jax.ShapeDtypeStruct(frames.shape, f32)]
+            + [jax.ShapeDtypeStruct(size, f32) for size in sizes],
+            in_specs=[chunk, whole((rows, chan))],
+            out_specs=[chunk] + [whole(size) for size in sizes],
+            compiler_params=pltpu.CompilerParams(vmem_limit_bytes=32 * 2**20),
+        )(grad_b, full)
+
     tiles = P(None, "row", "col", None)
     return jax.shard_map(
         shards,

time: 166 us -> 116 us (0.70)
  Pallas kernels: 158 us -> 112 us
  local copies, waits for them, and re-layouts: 7.39 us -> 2.58 us
    pallas_call x1 -> x2, Pallas kernels: 158 us -> 112 us  [the longest x1 108 us: shards(): pl.pallas_call(functools.partial(block_kernel, n_row, n_col), out_shape=[...]
    unnamed x13 -> x4, local copies, waits for them, and re-layouts: 7.39 us -> 2.58 us
where the time goes in v2:
time: 116 us; the launch traced here: 115 us
  Pallas kernels  112 us (97%)
  local copies, waits for them, and re-layouts  2.58 us (2%)
    pallas_call x1, Pallas kernels, shards(): pl.pallas_call(functools.partial(block_kernel, n_row, n_col), out_shape=[...  108 us
    pallas_call x1, Pallas kernels, shards(): pl.pallas_call(functools.partial(finish_kernel, factor), grid=(steps,), o...  3.86 us
    unnamed x4, local copies, waits for them, and re-layouts  2.58 us

profile of v2, /device:TPU:1, one launch (start us, length us, event | category | flops | bytes accessed | tf_op | source)
XLA Modules:
  0.0 115.4 jit_solution(6429526256186600759)
XLA Ops:
  0.6 108.3 %shard_map.128 = (bf16[16,32,16,128]{3,2,1,0:T(8,128)(2,1)}, bf16[1536,128]{1,0:T(8,128)(2,1)}) custom-call(bf16[16,32,16,128]{3,2,1,0:T(8,128)(2,1)} %frames_in.1, bf16[16,32,16,128]{3,2,1,0:T(8,128)(2,1)} %cotangent_in.1, f32[1,128]{1,0:T(1,128)} %bitcast.2, bf16[128,384]{1,0:T(8,128)(2,1)} %w_qkv.1, f32[4,256,256]{2,1,0:T(8,128)} %bias_in.1, ...), custom_call_target="tpu_custom_call" | custom-call | tf_op jit(solution)/shard_map/pallas_call | solution.py:490
  108.9 0.0 copy-start
  108.9 1.6 %copy-done = bf16[16,32,16,128]{3,2,1,0:T(8,128)(2,1)S(1)} copy-done((bf16[16,32,16,128]{3,2,1,0:T(8,128)(2,1)S(1)}, bf16[16,32,16,128]{3,2,1,0:T(8,128)(2,1)}, u32[]{:S(2)}) %copy-start) | copy-done | bytes 2097176
  110.5 0.0 copy-start.1
  110.5 1.0 copy-done.1
  111.5 3.9 %shard_map.129 = (f32[16,32,16,128]{3,2,1,0:T(8,128)}, f32[128,384]{1,0:T(8,128)}, f32[128,128]{1,0:T(8,128)}, f32[128,512]{1,0:T(8,128)}, f32[512,128]{1,0:T(8,128)}) custom-call(bf16[16,32,16,128]{3,2,1,0:T(8,128)(2,1)S(1)} %copy-done, bf16[1536,128]{1,0:T(8,128)(2,1)S(1)} %copy-done.1), custom_call_target="tpu_custom_call" | custom-call | tf_op jit(solution)/shard_map/pallas_call | solution.py:542
Async XLA Ops:
  108.9 1.6 %copy-start = (bf16[16,32,16,128]{3,2,1,0:T(8,128)(2,1)S(1)}, bf16[16,32,16,128]{3,2,1,0:T(8,128)(2,1)}, u32[]{:S(2)}) copy-start(bf16[16,32,16,128]{3,2,1,0:T(8,128)(2,1)} %get-tuple-element.7.grad_b) | copy-start | bytes 6291460
  110.5 1.0 copy-start.1

commit v3 on v2

--- a/solution.py
+++ b/solution.py
@@ -161,10 +161,10 @@
     frames_in, cotangent_in, gain1, w_qkv, bias_in, w_proj, gain2, w_up, w_down,
     grad, full_out,
     frames, cotangent, rel_bias,
-    to_left, to_up, to_diag, from_right, from_down, from_diag,
-    to_right, to_down, to_diag2, from_left, from_up, from_diag2,
+    to_side, to_row, to_corner, from_side, from_row, from_corner,
+    back_side, back_row, back_corner, got_side, got_row, got_corner,
     own_out, tile, probs, bias, gq, gp, gu, gd,
-    red, red_send, red_core, red_x, red_z, red_y, full,
+    red, red_send, red_core, red_plane, red_y, full,
     load_sem, in_send, in_recv, out_send, out_recv, grad_sem, red_ssem, red_rsem,
 ):
     nfr, tile_h, tile_w, chan = frames.shape
@@ -198,25 +198,23 @@
 
     left, right = lax.rem(col + n_col - 1, n_col), lax.rem(col + 1, n_col)
     up, down = lax.rem(row + n_row - 1, n_row), lax.rem(row + 1, n_row)
-    in_to = ((row, left), (up, col), (up, left))
-    out_to = ((row, right), (down, col), (down, right))
+    ways = (((row, left), (up, col), (up, left)), ((row, right), (down, col), (down, right)))
 
     def core_peer(s):
         return (row, col + 1 - 2 * core)
 
-    def x_peer(s):
-        return (row, (y_lo * n_x + lax.rem(x_at + s, n_x)) * 2 + core)
-
-    def z_peer(s):
-        return (y_hi * n_z + lax.rem(z_at + s, n_z), col)
+    plane_at = z_at * n_x + x_at
+
+    def plane_peer(s):
+        other = lax.rem(plane_at + s, n_x * n_z)
+        return (y_hi * n_z + other // n_x, (y_lo * n_x + lax.rem(other, n_x)) * 2 + core)
 
     def y_peer(s):
         other = lax.rem(y_at + s, n_y)
         return ((other // n_yl) * n_z + z_at, (lax.rem(other, n_yl) * n_x + x_at) * 2 + core)
 
-    peers = list(in_to) + list(out_to) + [core_peer(1)]
-    peers += [x_peer(s) for s in range(1, n_x)]
-    peers += [z_peer(s) for s in range(1, n_z)]
+    peers = list(ways[0]) + list(ways[1]) + [core_peer(1)]
+    peers += [plane_peer(s) for s in range(1, n_x * n_z)]
     peers += [y_peer(s) for s in range(1, n_y)]
     barrier = pltpu.get_barrier_semaphore()
     for peer in peers:
@@ -224,26 +222,26 @@
     pl.semaphore_wait(barrier, len(peers))
 
     def in_copies(s):
-        span = pl.ds(s * PER, PER)
-        pairs = ((to_left, from_right), (to_up, from_down), (to_diag, from_diag))
+        pairs = ((to_side, from_side), (to_row, from_row), (to_corner, from_corner))
         return [
             pltpu.make_async_remote_copy(
-                src_ref=a.at[span], dst_ref=b.at[span],
-                send_sem=in_send.at[i, s], recv_sem=in_recv.at[i, s],
-                device_id=in_to[i], device_id_type=MESH,
+                src_ref=a.at[s * PER + f], dst_ref=b.at[s * PER + f],
+                send_sem=in_send.at[i, s * PER + f], recv_sem=in_recv.at[i, s * PER + f],
+                device_id=ways[f][i], device_id_type=MESH,
             )
+            for f in range(PER)
             for i, (a, b) in enumerate(pairs)
         ]
 
     def out_copies(s):
-        span = pl.ds(s * PER, PER)
-        pairs = ((to_right, from_left), (to_down, from_up), (to_diag2, from_diag2))
+        pairs = ((back_side, got_side), (back_row, got_row), (back_corner, got_corner))
         return [
             pltpu.make_async_remote_copy(
-                src_ref=a.at[span], dst_ref=b.at[span],
-                send_sem=out_send.at[i, s], recv_sem=out_recv.at[i, s],
-                device_id=out_to[i], device_id_type=MESH,
+                src_ref=a.at[s * PER + f], dst_ref=b.at[s * PER + f],
+                send_sem=out_send.at[i, s * PER + f], recv_sem=out_recv.at[i, s * PER + f],
+                device_id=ways[1 - f][i], device_id_type=MESH,
             )
+            for f in range(PER)
             for i, (a, b) in enumerate(pairs)
         ]
 
@@ -252,13 +250,26 @@
             copy.wait()
         for f in range(PER):
             at = s * PER + f
+            rows_near, rows_far, cols_near, cols_far = cuts[f]
             for i, source in enumerate((frames, cotangent)):
                 whole = source[at].astype(f32)
-                to_left[at, i] = halves(whole[SHIFT:, :SHIFT])
-                to_up[at, i] = halves(whole[:SHIFT, SHIFT:])
-                to_diag[at, i] = halves(whole[:SHIFT, :SHIFT])
+                to_side[at, i] = halves(whole[rows_near, cols_far])
+                to_row[at, i] = halves(whole[rows_far, cols_near])
+                to_corner[at, i] = halves(whole[rows_far, cols_far])
         for copy in in_copies(s):
             copy.start()
+
+    keep = tile_h - SHIFT
+    cuts = (
+        (slice(SHIFT, None), slice(0, SHIFT), slice(SHIFT, None), slice(0, SHIFT)),
+        (slice(0, keep), slice(keep, None), slice(0, SHIFT), slice(SHIFT, None)),
+    )
+
+    def put(f, kept, side, over, corner):
+        order = (lambda a, b: (a, b)) if f == 0 else (lambda a, b: (b, a))
+        body = jnp.concatenate(order(kept, side), 1)
+        edge = jnp.concatenate(order(over, corner), 1)
+        return jnp.concatenate(order(body, edge), 0)
 
     def grad_copy(s):
         span = pl.ds(s * PER, PER)
@@ -269,15 +280,11 @@
             copy.wait_recv()
         for f in range(PER):
             at = s * PER + f
-            top = jnp.concatenate([unhalves(from_diag2[at]), unhalves(from_up[at])], 1)
-            tile[at, :SHIFT] = top.astype(bf16)
-            rest = jnp.concatenate([unhalves(from_left[at]), unhalves(own_out[at])], 1)
-            tile[at, SHIFT:] = rest.astype(bf16)
+            parts = (own_out, got_side, got_row, got_corner)
+            tile[at] = put(1 - f, *(unhalves(p[at]) for p in parts)).astype(bf16)
         grad_copy(s).start()
 
-    ahead = min(2, steps)
-    for s in range(ahead):
-        send_in(s)
+    send_in(0)
 
     bias_load.wait()
     wide = WS * WS
@@ -285,60 +292,74 @@
     at_k = lax.broadcasted_iota(jnp.int32, (wide, wide), 1)
     cut_row = (at_q // (WS * SHIFT)) != (at_k // (WS * SHIFT))
     cut_col = (lax.rem(at_q, WS) // SHIFT) != (lax.rem(at_k, WS) // SHIFT)
-    last_row = jnp.where(row == n_row - 1, 1.0, 0.0)
-    last_col = jnp.where(col == n_col - 1, 1.0, 0.0)
-    by_row = jnp.where(cut_row, last_row, 0.0)
-    by_col = jnp.where(cut_col, last_col, 0.0)
     windows = tile_h // WS
-    for w in range(windows):
-        cut = jnp.maximum(by_row, by_col) if w == windows - 1 else by_col
-        for h in range(HEADS):
-            bias[w, h] = (rel_bias[h] + cut * -100.0) * LOG2E
+    for f in range(PER):
+        last_row = jnp.where(row == (n_row - 1 if f == 0 else 0), 1.0, 0.0)
+        last_col = jnp.where(col == (n_col - 1 if f == 0 else 0), 1.0, 0.0)
+        by_row = jnp.where(cut_row, last_row, 0.0)
+        by_col = jnp.where(cut_col, last_col, 0.0)
+        for w in range(windows):
+            at_edge = w == (windows - 1 if f == 0 else 0)
+            cut = jnp.maximum(by_row, by_col) if at_edge else by_col
+            for h in range(HEADS):
+                bias[f, w, h] = (rel_bias[h] + cut * -100.0) * LOG2E
     for ref in (gq, gp, gu, gd):
         ref[...] = jnp.zeros_like(ref)
 
-    def step(s, carry):
-        @pl.when(s + ahead < steps)
-        def _():
-            send_in(s + ahead)
-
+    def arrive(s):
         for copy in in_copies(s):
             copy.wait_recv()
+
+    arrive(0)
+    if steps > 1:
+        send_in(1)
+
+    def step(s, carry):
+        @pl.when(s + 2 < steps)
+        def _():
+            send_in(s + 2)
+
         stages, result = [], [None] * (PER * windows)
         for f in range(PER):
             at = s * PER + f
             parts = []
             for i, source in enumerate((frames, cotangent)):
-                own = source[at].astype(f32)[SHIFT:, SHIFT:]
-                first = jnp.concatenate([own, unhalves(from_down[at, i])], 0)
-                second = jnp.concatenate(
-                    [unhalves(from_right[at, i]), unhalves(from_diag[at, i])], 0
-                )
-                parts.append(jnp.concatenate([first, second], 1))
+                own = source[at].astype(f32)[cuts[f][0], cuts[f][2]]
+                got = (unhalves(p[at, i]) for p in (from_side, from_row, from_corner))
+                parts.append(put(f, own, *got))
             for w in range(windows):
                 x, c = (p[w * WS : (w + 1) * WS].reshape(wide, chan) for p in parts)
                 stages.append(
                     window_block(
-                        f * windows + w, x, c, bias.at[w], gain1[...], gain2[...],
+                        f * windows + w, x, c, bias.at[f, w], gain1[...], gain2[...],
                         w_qkv, w_proj, w_up, w_down, probs, (gq, gp, gu, gd), result,
                     )
                 )
         take_turns(stages)
-        keep = tile_h - SHIFT
         for f in range(PER):
             at = s * PER + f
             out = [r.reshape(WS, WS, chan) for r in result[f * windows : (f + 1) * windows]]
             out = jnp.concatenate(out, 0)
-            to_right[at] = halves(out[:keep, SHIFT:])
-            to_down[at] = halves(out[keep:, :SHIFT])
-            to_diag2[at] = halves(out[keep:, SHIFT:])
-            own_out[at] = halves(out[:keep, :SHIFT])
+            if f == 0:
+                rows_own, rows_far = slice(0, keep), slice(keep, None)
+                cols_own, cols_far = slice(0, SHIFT), slice(SHIFT, None)
+            else:
+                rows_own, rows_far = slice(SHIFT, None), slice(0, SHIFT)
+                cols_own, cols_far = slice(SHIFT, None), slice(0, SHIFT)
+            back_side[at] = halves(out[rows_own, cols_far])
+            back_row[at] = halves(out[rows_far, cols_own])
+            back_corner[at] = halves(out[rows_far, cols_far])
+            own_out[at] = halves(out[rows_own, cols_own])
         for copy in out_copies(s):
             copy.start()
 
         @pl.when(s >= 1)
         def _():
             finish(s - 1)
+
+        @pl.when(s + 1 < steps)
+        def _():
+            arrive(s + 1)
 
         return carry
 
@@ -352,8 +373,7 @@
         red[chan * (8 + j) : chan * (9 + j)] = gd[:, chan * j : chan * (j + 1)]
     rows = red.shape[0]
     size_c = rows // 2
-    size_x = size_c // n_x
-    size_z = size_x // n_z
+    size_z = size_c // (n_x * n_z)
 
     def copy_to(peer, src, dst, sem):
         return pltpu.make_async_remote_copy(
@@ -399,9 +419,8 @@
         return base, sem
 
     landings = []
-    red_stage = (full.at[pl.ds(rows, size_c)], full.at[pl.ds(rows + size_c, size_x)])
-    base, sem = reduce_stage(base, size_x, n_x, x_at, x_peer, red_x, sem)
-    base, sem = reduce_stage(base, size_z, n_z, z_at, z_peer, red_z, sem)
+    red_stage = (full.at[pl.ds(rows, size_c)],)
+    base, sem = reduce_stage(base, size_z, n_x * n_z, plane_at, plane_peer, red_plane, sem)
     red_y[y_at] = red[at(base, size_z)].astype(bf16)
     started = []
     for s in range(1, n_y):
@@ -428,8 +447,7 @@
         copies.extend(started)
         return sem
 
-    sem = gather_stage(base, size_z, n_z, z_peer, sem)
-    sem = gather_stage(core * size_c + x_at * size_x, size_x, n_x, x_peer, sem)
+    sem = gather_stage(base, size_z, n_x * n_z, plane_peer, sem)
     sem = gather_stage(core * size_c, size_c, 2, core_peer, sem)
     full_out[...] = full[:rows]
     for copy in copies:
@@ -475,9 +493,8 @@
         n_z, n_x = min(4, n_row), min(4, n_col // 2)
         n_y = (n_row // n_z) * (n_col // (2 * n_x))
         size_c = rows // 2
-        size_x = size_c // n_x
-        size_z = size_x // n_z
-        n_sem = 2 + 2 * (n_x - 1) + 2 * (n_z - 1) + (n_y - 1)
+        size_z = size_c // (n_x * n_z)
+        n_sem = 2 + 2 * (n_x * n_z - 1) + (n_y - 1)
 
         def pieces(k):
             sizes = (long, short, short)
@@ -505,7 +522,7 @@
                 pltpu.VMEM((nfr, long, 2 * SHIFT, chan), bf16),
                 pltpu.VMEM(frames.shape, bf16),
                 pltpu.VMEM((PER * windows, HEADS, wide, wide), bf16),
-                pltpu.VMEM((windows, HEADS, wide, wide), f32),
+                pltpu.VMEM((PER, windows, HEADS, wide, wide), f32),
                 pltpu.VMEM((chan, 3 * chan), f32),
                 pltpu.VMEM((chan, chan), f32),
                 pltpu.VMEM((chan, ff), f32),
@@ -513,15 +530,14 @@
                 pltpu.VMEM((rows, chan), f32),
                 pltpu.VMEM((rows, chan), bf16),
                 pltpu.VMEM((size_c, chan), bf16),
-                pltpu.VMEM((max(n_x - 1, 1), size_x, chan), bf16),
-                pltpu.VMEM((max(n_z - 1, 1), size_z, chan), bf16),
+                pltpu.VMEM((n_x * n_z - 1, size_z, chan), bf16),
                 pltpu.VMEM((n_y, size_z, chan), bf16),
-                pltpu.VMEM((rows + size_c + size_x, chan), bf16),
+                pltpu.VMEM((rows + size_c, chan), bf16),
                 pltpu.SemaphoreType.DMA((2, steps + 1)),
-                pltpu.SemaphoreType.DMA((3, steps)),
-                pltpu.SemaphoreType.DMA((3, steps)),
-                pltpu.SemaphoreType.DMA((3, steps)),
-                pltpu.SemaphoreType.DMA((3, steps)),
+                pltpu.SemaphoreType.DMA((3, nfr)),
+                pltpu.SemaphoreType.DMA((3, nfr)),
+                pltpu.SemaphoreType.DMA((3, nfr)),
+                pltpu.SemaphoreType.DMA((3, nfr)),
                 pltpu.SemaphoreType.DMA((steps,)),
                 pltpu.SemaphoreType.DMA((n_sem,)),
                 pltpu.SemaphoreType.DMA((n_sem,)),
@@ -546,7 +562,7 @@
             + [jax.ShapeDtypeStruct(size, f32) for size in sizes],
             in_specs=[chunk, whole((rows, chan))],
             out_specs=[chunk] + [whole(size) for size in sizes],
-            compiler_params=pltpu.CompilerParams(vmem_limit_bytes=32 * 2**20),
+            compiler_params=pltpu.CompilerParams(vmem_limit_bytes=60 * 2**20),
         )(grad_b, full)
 
     tiles = P(None, "row", "col", None)

time: 116 us -> 109 us (0.940)
  Pallas kernels: 112 us -> 108 us
  local copies, waits for them, and re-layouts: 2.58 us -> 0 us
    pallas_call x1, Pallas kernels: 108 us -> 102 us  [shards(): pl.pallas_call(functools.partial(block_kernel, n_row, n_col), out_shape=[...]
    pallas_call x1, Pallas kernels: 3.86 us -> 6.54 us  [shards(): pl.pallas_call(functools.partial(finish_kernel, factor), grid=(steps,), o...]
    unnamed x4 -> x0, local copies, waits for them, and re-layouts: 2.58 us -> none
where the time goes in v3:
time: 109 us
  Pallas kernels  108 us (99%)
    pallas_call x1, Pallas kernels, shards(): pl.pallas_call(functools.partial(block_kernel, n_row, n_col), out_shape=[...  102 us
    pallas_call x1, Pallas kernels, shards(): pl.pallas_call(functools.partial(finish_kernel, factor), grid=(steps,), o...  6.54 us

profile of v3, /device:TPU:1, one launch (start us, length us, event | category | flops | bytes accessed | tf_op | source)
XLA Modules:
  0.0 109.0 jit_solution(14609175921454436051)
XLA Ops:
  0.6 101.8 %shard_map.128 = (bf16[16,32,16,128]{3,2,1,0:T(8,128)(2,1)}, bf16[1536,128]{1,0:T(8,128)(2,1)}) custom-call(bf16[16,32,16,128]{3,2,1,0:T(8,128)(2,1)} %frames_in.1, bf16[16,32,16,128]{3,2,1,0:T(8,128)(2,1)} %cotangent_in.1, f32[1,128]{1,0:T(1,128)} %bitcast.2, bf16[128,384]{1,0:T(8,128)(2,1)} %w_qkv.1, f32[4,256,256]{2,1,0:T(8,128)} %bias_in.1, ...), custom_call_target="tpu_custom_call" | custom-call | tf_op jit(solution)/shard_map/pallas_call | solution.py:507
  102.4 6.5 %shard_map.129 = (f32[16,32,16,128]{3,2,1,0:T(8,128)}, f32[128,384]{1,0:T(8,128)}, f32[128,128]{1,0:T(8,128)}, f32[128,512]{1,0:T(8,128)}, f32[512,128]{1,0:T(8,128)}) custom-call(bf16[16,32,16,128]{3,2,1,0:T(8,128)(2,1)} %get-tuple-element.7.grad_b, bf16[1536,128]{1,0:T(8,128)(2,1)} %get-tuple-element.8.full), custom_call_target="tpu_custom_call" | custom-call | tf_op jit(solution)/shard_map/pallas_call | solution.py:558

commit v4 on v3

--- a/solution.py
+++ b/solution.py
@@ -40,10 +40,11 @@
 
 def gelu_and_slope(u):
     expo = jnp.exp2(u * u * (-0.5 * LOG2E))
-    t = 1.0 / (1.0 + (0.3275911 / math.sqrt(2.0)) * jnp.abs(u))
-    poly = 0.5 * 1.061405429
-    for c in (-1.453152027, 1.421413741, -0.284496736, 0.254829592):
-        poly = t * poly + 0.5 * c
+    p = math.sqrt(2.0) / 0.3275911
+    t = 1.0 / (jnp.abs(u) + p)
+    poly = 0.5 * 1.061405429 * p**5
+    for n, c in ((4, -1.453152027), (3, 1.421413741), (2, -0.284496736), (1, 0.254829592)):
+        poly = t * poly + 0.5 * c * p**n
     tail = t * poly * expo
     cdf = jnp.where(u < 0.0, tail, 1.0 - tail)
     return u * cdf, cdf + u * expo * (1.0 / math.sqrt(2.0 * math.pi))
@@ -219,7 +220,6 @@
     barrier = pltpu.get_barrier_semaphore()
     for peer in peers:
         pl.semaphore_signal(barrier, inc=1, device_id=peer, device_id_type=MESH)
-    pl.semaphore_wait(barrier, len(peers))
 
     def in_copies(s):
         pairs = ((to_side, from_side), (to_row, from_row), (to_corner, from_corner))
@@ -245,7 +245,7 @@
             for i, (a, b) in enumerate(pairs)
         ]
 
-    def send_in(s):
+    def pack_in(s):
         for copy in loads(s):
             copy.wait()
         for f in range(PER):
@@ -256,6 +256,9 @@
                 to_side[at, i] = halves(whole[rows_near, cols_far])
                 to_row[at, i] = halves(whole[rows_far, cols_near])
                 to_corner[at, i] = halves(whole[rows_far, cols_far])
+
+    def send_in(s):
+        pack_in(s)
         for copy in in_copies(s):
             copy.start()
 
@@ -284,7 +287,10 @@
             tile[at] = put(1 - f, *(unhalves(p[at]) for p in parts)).astype(bf16)
         grad_copy(s).start()
 
-    send_in(0)
+    pack_in(0)
+    pl.semaphore_wait(barrier, len(peers))
+    for copy in in_copies(0):
+        copy.start()
 
     bias_load.wait()
     wide = WS * WS
@@ -310,9 +316,9 @@
         for copy in in_copies(s):
             copy.wait_recv()
 
-    arrive(0)
     if steps > 1:
         send_in(1)
+    arrive(0)
 
     def step(s, carry):
         @pl.when(s + 2 < steps)
@@ -353,9 +359,9 @@
         for copy in out_copies(s):
             copy.start()
 
-        @pl.when(s >= 1)
+        @pl.when(s >= 2)
         def _():
-            finish(s - 1)
+            finish(s - 2)
 
         @pl.when(s + 1 < steps)
         def _():
@@ -392,7 +398,8 @@
     first.start()
     copies.append(first)
     sem += 1
-    finish(steps - 1)
+    if steps > 1:
+        finish(steps - 2)
     first.wait_recv()
     red[at(base, size_c)] += red_core[...].astype(f32)
 
@@ -427,6 +434,7 @@
         started.append(copy_to(y_peer(s), red_y.at[y_at], red_y.at[y_at], sem))
         started[-1].start()
         sem += 1
+    finish(steps - 1)
     for copy in started:
         copy.wait_recv()
     copies.extend(started)
@@ -462,22 +470,38 @@
     lax.fori_loop(0, steps, drain, 0)
 
 
-def finish_kernel(factor, grad_b, full, grad, g_qkv, g_proj, g_up, g_down):
-    grad[...] = grad_b[...].astype(f32)
-
-    @pl.when(pl.program_id(0) == 0)
-    def _():
-        chan = full.shape[1]
-
-        def block(j):
-            return full[chan * j : chan * (j + 1)].astype(f32) * factor
-
-        for j in range(g_qkv.shape[1] // chan):
-            g_qkv[:, chan * j : chan * (j + 1)] = block(j)
-        g_proj[...] = block(3)
-        for j in range(g_up.shape[1] // chan):
-            g_up[:, chan * j : chan * (j + 1)] = block(4 + j)
-            g_down[chan * j : chan * (j + 1)] = block(8 + j).T
+def finish_kernel(
+    factor, grad_b, full, grad, g_qkv, g_proj, g_up, g_down, narrow, wide, load_sem, store_sem
+):
+    steps = load_sem.shape[0]
+    per = narrow.shape[0] // steps
+    chan = full.shape[1]
+
+    def load(s):
+        span = pl.ds(s * per, per)
+        return pltpu.make_async_copy(grad_b.at[span], narrow.at[span], load_sem.at[s])
+
+    def store(s):
+        span = pl.ds(s * per, per)
+        return pltpu.make_async_copy(wide.at[span], grad.at[span], store_sem.at[s])
+
+    def block(j):
+        return full[chan * j : chan * (j + 1)].astype(f32) * factor
+
+    for s in range(steps):
+        load(s).start()
+    for j in range(g_qkv.shape[1] // chan):
+        g_qkv[:, chan * j : chan * (j + 1)] = block(j)
+    g_proj[...] = block(3)
+    for j in range(g_up.shape[1] // chan):
+        g_up[:, chan * j : chan * (j + 1)] = block(4 + j)
+        g_down[chan * j : chan * (j + 1)] = block(8 + j).T
+    for s in range(steps):
+        load(s).wait()
+        wide[per * s : per * (s + 1)] = narrow[per * s : per * (s + 1)].astype(f32)
+        store(s).start()
+    for s in range(steps):
+        store(s).wait()
 
 
 def solution(mesh):
@@ -550,19 +574,20 @@
             gain2.reshape(1, chan), w_up, w_down,
         )
 
-        def whole(shape):
-            return pl.BlockSpec(shape, lambda i: (0, 0))
-
-        chunk = pl.BlockSpec((PER,) + frames.shape[1:], lambda i: (i, 0, 0, 0))
         sizes = [(chan, 3 * chan), (chan, chan), (chan, ff), (ff, chan)]
         return pl.pallas_call(
             functools.partial(finish_kernel, factor),
-            grid=(steps,),
             out_shape=[jax.ShapeDtypeStruct(frames.shape, f32)]
             + [jax.ShapeDtypeStruct(size, f32) for size in sizes],
-            in_specs=[chunk, whole((rows, chan))],
-            out_specs=[chunk] + [whole(size) for size in sizes],
-            compiler_params=pltpu.CompilerParams(vmem_limit_bytes=60 * 2**20),
+            in_specs=[hbm, vmem],
+            out_specs=[hbm] + [vmem] * 4,
+            scratch_shapes=[
+                pltpu.VMEM(frames.shape, bf16),
+                pltpu.VMEM(frames.shape, f32),
+                pltpu.SemaphoreType.DMA((steps,)),
+                pltpu.SemaphoreType.DMA((steps,)),
+            ],
+            compiler_params=pltpu.CompilerParams(vmem_limit_bytes=56 * 2**20),
         )(grad_b, full)
 
     tiles = P(None, "row", "col", None)

time: 109 us -> 104 us (0.954)
  Pallas kernels: 108 us -> 103 us
    pallas_call x1, Pallas kernels: 102 us -> 98.2 us  [shards(): pl.pallas_call(functools.partial(block_kernel, n_row, n_col), out_shape=[...]
    pallas_call x1, Pallas kernels: 6.54 us -> 5 us  [shards(): pl.pallas_call(functools.partial(finish_kernel, factor), out_shape=[jax.S...]
where the time goes in v4:
time: 104 us
  Pallas kernels  103 us (99%)
    pallas_call x1, Pallas kernels, shards(): pl.pallas_call(functools.partial(block_kernel, n_row, n_col), out_shape=[...  98.2 us
    pallas_call x1, Pallas kernels, shards(): pl.pallas_call(functools.partial(finish_kernel, factor), out_shape=[jax.S...  5 us

profile of v4, /device:TPU:1, one launch (start us, length us, event | category | flops | bytes accessed | tf_op | source)
XLA Modules:
  0.0 103.8 jit_solution(12623672145909424210)
XLA Ops:
  0.6 98.2 %shard_map.128 = (bf16[16,32,16,128]{3,2,1,0:T(8,128)(2,1)}, bf16[1536,128]{1,0:T(8,128)(2,1)}) custom-call(bf16[16,32,16,128]{3,2,1,0:T(8,128)(2,1)} %frames_in.1, bf16[16,32,16,128]{3,2,1,0:T(8,128)(2,1)} %cotangent_in.1, f32[1,128]{1,0:T(1,128)} %bitcast.2, bf16[128,384]{1,0:T(8,128)(2,1)} %w_qkv.1, f32[4,256,256]{2,1,0:T(8,128)} %bias_in.1, ...), custom_call_target="tpu_custom_call" | custom-call | tf_op jit(solution)/shard_map/pallas_call | solution.py:531
  98.8 5.0 %shard_map.129 = (f32[16,32,16,128]{3,2,1,0:T(8,128)}, f32[128,384]{1,0:T(8,128)}, f32[128,128]{1,0:T(8,128)}, f32[128,512]{1,0:T(8,128)}, f32[512,128]{1,0:T(8,128)}) custom-call(bf16[16,32,16,128]{3,2,1,0:T(8,128)(2,1)} %get-tuple-element.7.grad_b, bf16[1536,128]{1,0:T(8,128)(2,1)} %get-tuple-element.8.full), custom_call_target="tpu_custom_call" | custom-call | tf_op jit(solution)/shard_map/pallas_call | solution.py:578

commit v5 on v4

--- a/solution.py
+++ b/solution.py
@@ -16,7 +16,7 @@
 MESH = pl.DeviceIdType.MESH
 bf16 = jnp.bfloat16
 f32 = jnp.float32
-PER = 2
+PER = 4
 
 
 def dot(a, b, ca, cb):
@@ -227,7 +227,7 @@
             pltpu.make_async_remote_copy(
                 src_ref=a.at[s * PER + f], dst_ref=b.at[s * PER + f],
                 send_sem=in_send.at[i, s * PER + f], recv_sem=in_recv.at[i, s * PER + f],
-                device_id=ways[f][i], device_id_type=MESH,
+                device_id=ways[f % 2][i], device_id_type=MESH,
             )
             for f in range(PER)
             for i, (a, b) in enumerate(pairs)
@@ -239,7 +239,7 @@
             pltpu.make_async_remote_copy(
                 src_ref=a.at[s * PER + f], dst_ref=b.at[s * PER + f],
                 send_sem=out_send.at[i, s * PER + f], recv_sem=out_recv.at[i, s * PER + f],
-                device_id=ways[1 - f][i], device_id_type=MESH,
+                device_id=ways[1 - f % 2][i], device_id_type=MESH,
             )
             for f in range(PER)
             for i, (a, b) in enumerate(pairs)
@@ -250,7 +250,7 @@
             copy.wait()
         for f in range(PER):
             at = s * PER + f
-            rows_near, rows_far, cols_near, cols_far = cuts[f]
+            rows_near, rows_far, cols_near, cols_far = cuts[f % 2]
             for i, source in enumerate((frames, cotangent)):
                 whole = source[at].astype(f32)
                 to_side[at, i] = halves(whole[rows_near, cols_far])
@@ -284,7 +284,7 @@
         for f in range(PER):
             at = s * PER + f
             parts = (own_out, got_side, got_row, got_corner)
-            tile[at] = put(1 - f, *(unhalves(p[at]) for p in parts)).astype(bf16)
+            tile[at] = put(1 - f % 2, *(unhalves(p[at]) for p in parts)).astype(bf16)
         grad_copy(s).start()
 
     pack_in(0)
@@ -299,7 +299,7 @@
     cut_row = (at_q // (WS * SHIFT)) != (at_k // (WS * SHIFT))
     cut_col = (lax.rem(at_q, WS) // SHIFT) != (lax.rem(at_k, WS) // SHIFT)
     windows = tile_h // WS
-    for f in range(PER):
+    for f in range(2):
         last_row = jnp.where(row == (n_row - 1 if f == 0 else 0), 1.0, 0.0)
         last_col = jnp.where(col == (n_col - 1 if f == 0 else 0), 1.0, 0.0)
         by_row = jnp.where(cut_row, last_row, 0.0)
@@ -317,8 +317,11 @@
             copy.wait_recv()
 
     if steps > 1:
-        send_in(1)
+        pack_in(1)
     arrive(0)
+    if steps > 1:
+        for copy in in_copies(1):
+            copy.start()
 
     def step(s, carry):
         @pl.when(s + 2 < steps)
@@ -330,14 +333,14 @@
             at = s * PER + f
             parts = []
             for i, source in enumerate((frames, cotangent)):
-                own = source[at].astype(f32)[cuts[f][0], cuts[f][2]]
+                own = source[at].astype(f32)[cuts[f % 2][0], cuts[f % 2][2]]
                 got = (unhalves(p[at, i]) for p in (from_side, from_row, from_corner))
-                parts.append(put(f, own, *got))
+                parts.append(put(f % 2, own, *got))
             for w in range(windows):
                 x, c = (p[w * WS : (w + 1) * WS].reshape(wide, chan) for p in parts)
                 stages.append(
                     window_block(
-                        f * windows + w, x, c, bias.at[f, w], gain1[...], gain2[...],
+                        f * windows + w, x, c, bias.at[f % 2, w], gain1[...], gain2[...],
                         w_qkv, w_proj, w_up, w_down, probs, (gq, gp, gu, gd), result,
                     )
                 )
@@ -346,7 +349,7 @@
             at = s * PER + f
             out = [r.reshape(WS, WS, chan) for r in result[f * windows : (f + 1) * windows]]
             out = jnp.concatenate(out, 0)
-            if f == 0:
+            if f % 2 == 0:
                 rows_own, rows_far = slice(0, keep), slice(keep, None)
                 cols_own, cols_far = slice(0, SHIFT), slice(SHIFT, None)
             else:
@@ -471,7 +474,8 @@
 
 
 def finish_kernel(
-    factor, grad_b, full, grad, g_qkv, g_proj, g_up, g_down, narrow, wide, load_sem, store_sem
+    factor, grad_b, full_in, grad, qkv_out, proj_out, up_out, down_out,
+    narrow, wide, full, g_qkv, g_proj, g_up, g_down, load_sem, store_sem, full_sem, sum_sem,
 ):
     steps = load_sem.shape[0]
     per = narrow.shape[0] // steps
@@ -488,20 +492,29 @@
     def block(j):
         return full[chan * j : chan * (j + 1)].astype(f32) * factor
 
+    full_load = pltpu.make_async_copy(full_in, full, full_sem)
     for s in range(steps):
         load(s).start()
+    full_load.start()
+    for s in range(steps):
+        load(s).wait()
+        wide[per * s : per * (s + 1)] = narrow[per * s : per * (s + 1)].astype(f32)
+        store(s).start()
+    full_load.wait()
     for j in range(g_qkv.shape[1] // chan):
         g_qkv[:, chan * j : chan * (j + 1)] = block(j)
     g_proj[...] = block(3)
     for j in range(g_up.shape[1] // chan):
         g_up[:, chan * j : chan * (j + 1)] = block(4 + j)
         g_down[chan * j : chan * (j + 1)] = block(8 + j).T
-    for s in range(steps):
-        load(s).wait()
-        wide[per * s : per * (s + 1)] = narrow[per * s : per * (s + 1)].astype(f32)
-        store(s).start()
+    pairs = ((g_qkv, qkv_out), (g_proj, proj_out), (g_up, up_out), (g_down, down_out))
+    sums = [pltpu.make_async_copy(a, b, sum_sem.at[i]) for i, (a, b) in enumerate(pairs)]
+    for copy in sums:
+        copy.start()
     for s in range(steps):
         store(s).wait()
+    for copy in sums:
+        copy.wait()
 
 
 def solution(mesh):
@@ -546,7 +559,7 @@
                 pltpu.VMEM((nfr, long, 2 * SHIFT, chan), bf16),
                 pltpu.VMEM(frames.shape, bf16),
                 pltpu.VMEM((PER * windows, HEADS, wide, wide), bf16),
-                pltpu.VMEM((PER, windows, HEADS, wide, wide), f32),
+                pltpu.VMEM((2, windows, HEADS, wide, wide), f32),
                 pltpu.VMEM((chan, 3 * chan), f32),
                 pltpu.VMEM((chan, chan), f32),
                 pltpu.VMEM((chan, ff), f32),
@@ -579,13 +592,19 @@
             functools.partial(finish_kernel, factor),
             out_shape=[jax.ShapeDtypeStruct(frames.shape, f32)]
             + [jax.ShapeDtypeStruct(size, f32) for size in sizes],
-            in_specs=[hbm, vmem],
-            out_specs=[hbm] + [vmem] * 4,
+            in_specs=[hbm, hbm],
+            out_specs=[hbm] * 5,
             scratch_shapes=[
                 pltpu.VMEM(frames.shape, bf16),
                 pltpu.VMEM(frames.shape, f32),
-                pltpu.SemaphoreType.DMA((steps,)),
-                pltpu.SemaphoreType.DMA((steps,)),
+                pltpu.VMEM((rows, chan), bf16),
+            ]
+            + [pltpu.VMEM(size, f32) for size in sizes]
+            + [
+                pltpu.SemaphoreType.DMA((nfr // 2,)),
+                pltpu.SemaphoreType.DMA((nfr // 2,)),
+                pltpu.SemaphoreType.DMA,
+                pltpu.SemaphoreType.DMA((4,)),
             ],
             compiler_params=pltpu.CompilerParams(vmem_limit_bytes=56 * 2**20),
         )(grad_b, full)

time: 104 us -> 98.3 us (0.945)
  Pallas kernels: 103 us -> 97.5 us
    pallas_call x1, Pallas kernels: 98.2 us -> 94.1 us  [shards(): pl.pallas_call(functools.partial(block_kernel, n_row, n_col), out_shape=[...]
    pallas_call x1, Pallas kernels: 5 us -> 3.41 us  [shards(): pl.pallas_call(functools.partial(finish_kernel, factor), out_shape=[jax.S...]
where the time goes in v5:
time: 98.3 us; the launch traced here: 98.2 us
  Pallas kernels  97.5 us (99%)
    pallas_call x1, Pallas kernels, shards(): pl.pallas_call(functools.partial(block_kernel, n_row, n_col), out_shape=[...  94.1 us
    pallas_call x1, Pallas kernels, shards(): pl.pallas_call(functools.partial(finish_kernel, factor), out_shape=[jax.S...  3.41 us

profile of v5, /device:TPU:1, one launch (start us, length us, event | category | flops | bytes accessed | tf_op | source)
XLA Modules:
  0.0 98.2 jit_solution(924966878146358747)
XLA Ops:
  0.6 94.1 %shard_map.128 = (bf16[16,32,16,128]{3,2,1,0:T(8,128)(2,1)}, bf16[1536,128]{1,0:T(8,128)(2,1)}) custom-call(bf16[16,32,16,128]{3,2,1,0:T(8,128)(2,1)} %frames_in.1, bf16[16,32,16,128]{3,2,1,0:T(8,128)(2,1)} %cotangent_in.1, f32[1,128]{1,0:T(1,128)} %bitcast.2, bf16[128,384]{1,0:T(8,128)(2,1)} %w_qkv.1, f32[4,256,256]{2,1,0:T(8,128)} %bias_in.1, ...), custom_call_target="tpu_custom_call" | custom-call | tf_op jit(solution)/shard_map/pallas_call | solution.py:544
  94.8 3.4 %shard_map.129 = (f32[16,32,16,128]{3,2,1,0:T(8,128)}, f32[128,384]{1,0:T(8,128)}, f32[128,128]{1,0:T(8,128)}, f32[128,512]{1,0:T(8,128)}, f32[512,128]{1,0:T(8,128)}) custom-call(bf16[16,32,16,128]{3,2,1,0:T(8,128)(2,1)} %get-tuple-element.7.grad_b, bf16[1536,128]{1,0:T(8,128)(2,1)} %get-tuple-element.8.full_in), custom_call_target="tpu_custom_call" | custom-call | tf_op jit(solution)/shard_map/pallas_call | solution.py:591

commit v6 on v5

--- a/solution.py
+++ b/solution.py
@@ -145,8 +145,11 @@
 
 
 def take_turns(stages):
-    while stages:
-        stages = [one for one in stages if next(one, stages) is not stages]
+    waiting, running = list(stages), []
+    while waiting or running:
+        if waiting:
+            running.append(waiting.pop(0))
+        running = [one for one in running if next(one, running) is not running]
 
 
 def halves(tile):
@@ -259,7 +262,7 @@
 
     def send_in(s):
         pack_in(s)
-        for copy in in_copies(s):
+        for copy in reversed(in_copies(s)):
             copy.start()
 
     keep = tile_h - SHIFT
@@ -289,7 +292,7 @@
 
     pack_in(0)
     pl.semaphore_wait(barrier, len(peers))
-    for copy in in_copies(0):
+    for copy in reversed(in_copies(0)):
         copy.start()
 
     bias_load.wait()
@@ -320,7 +323,7 @@
         pack_in(1)
     arrive(0)
     if steps > 1:
-        for copy in in_copies(1):
+        for copy in reversed(in_copies(1)):
             copy.start()
 
     def step(s, carry):
@@ -359,7 +362,7 @@
             back_row[at] = halves(out[rows_far, cols_own])
             back_corner[at] = halves(out[rows_far, cols_far])
             own_out[at] = halves(out[rows_own, cols_own])
-        for copy in out_copies(s):
+        for copy in reversed(out_copies(s)):
             copy.start()
 
         @pl.when(s >= 2)

time: 98.3 us -> 97.6 us (level)
  no operation moved by 1% of the time
where the time goes in v6:
time: 97.6 us; the launch traced here: 97.5 us
  Pallas kernels  96.8 us (99%)
    pallas_call x1, Pallas kernels, shards(): pl.pallas_call(functools.partial(block_kernel, n_row, n_col), out_shape=[...  93.4 us
    pallas_call x1, Pallas kernels, shards(): pl.pallas_call(functools.partial(finish_kernel, factor), out_shape=[jax.S...  3.41 us

profile of v6, /device:TPU:1, one launch (start us, length us, event | category | flops | bytes accessed | tf_op | source)
XLA Modules:
  0.0 97.5 jit_solution(4262711577562521709)
XLA Ops:
  0.6 93.4 %shard_map.128 = (bf16[16,32,16,128]{3,2,1,0:T(8,128)(2,1)}, bf16[1536,128]{1,0:T(8,128)(2,1)}) custom-call(bf16[16,32,16,128]{3,2,1,0:T(8,128)(2,1)} %frames_in.1, bf16[16,32,16,128]{3,2,1,0:T(8,128)(2,1)} %cotangent_in.1, f32[1,128]{1,0:T(1,128)} %bitcast.2, bf16[128,384]{1,0:T(8,128)(2,1)} %w_qkv.1, f32[4,256,256]{2,1,0:T(8,128)} %bias_in.1, ...), custom_call_target="tpu_custom_call" | custom-call | tf_op jit(solution)/shard_map/pallas_call | solution.py:547
  94.1 3.4 %shard_map.129 = (f32[16,32,16,128]{3,2,1,0:T(8,128)}, f32[128,384]{1,0:T(8,128)}, f32[128,128]{1,0:T(8,128)}, f32[128,512]{1,0:T(8,128)}, f32[512,128]{1,0:T(8,128)}) custom-call(bf16[16,32,16,128]{3,2,1,0:T(8,128)(2,1)} %get-tuple-element.7.grad_b, bf16[1536,128]{1,0:T(8,128)(2,1)} %get-tuple-element.8.full_in), custom_call_target="tpu_custom_call" | custom-call | tf_op jit(solution)/shard_map/pallas_call | solution.py:594

commit v7 on v6

--- a/solution.py
+++ b/solution.py
@@ -404,6 +404,17 @@
     first.start()
     copies.append(first)
     sem += 1
+
+    def drain_in(s, carry):
+        for copy in in_copies(s):
+            copy.wait_send()
+        return carry
+
+    def drain_out(s, carry):
+        for copy in out_copies(s):
+            copy.wait_send()
+        return carry
+
     if steps > 1:
         finish(steps - 2)
     first.wait_recv()
@@ -422,6 +433,7 @@
             started[-1].start()
             sem += 1
         base = base + index * size
+        lax.fori_loop(0, nfr // PER, drain_in, 0)
         for copy in started:
             copy.wait_recv()
         total = red[at(base, size)]
@@ -441,6 +453,7 @@
         started[-1].start()
         sem += 1
     finish(steps - 1)
+    lax.fori_loop(0, steps, drain_out, 0)
     for copy in started:
         copy.wait_recv()
     copies.extend(started)
@@ -456,6 +469,8 @@
             started.append(copy_to(peer(s), part, part, sem))
             started[-1].start()
             sem += 1
+        while copies:
+            copies.pop().wait_send()
         for copy in started:
             copy.wait_recv()
         copies.extend(started)
@@ -468,8 +483,6 @@
         copy.wait_send()
 
     def drain(s, carry):
-        for copy in in_copies(s) + out_copies(s):
-            copy.wait_send()
         grad_copy(s).wait()
         return carry
 

time: 97.6 us -> 97.4 us (level)
  no operation moved by 1% of the time
where the time goes in v7:
time: 97.4 us; the launch traced here: 97.3 us
  Pallas kernels  96.6 us (99%)
    pallas_call x1, Pallas kernels, shards(): pl.pallas_call(functools.partial(block_kernel, n_row, n_col), out_shape=[...  93.2 us
    pallas_call x1, Pallas kernels, shards(): pl.pallas_call(functools.partial(finish_kernel, factor), out_shape=[jax.S...  3.41 us

profile of v7, /device:TPU:1, one launch (start us, length us, event | category | flops | bytes accessed | tf_op | source)
XLA Modules:
  0.0 97.3 jit_solution(7262789714565342856)
XLA Ops:
  0.6 93.2 %shard_map.128 = (bf16[16,32,16,128]{3,2,1,0:T(8,128)(2,1)}, bf16[1536,128]{1,0:T(8,128)(2,1)}) custom-call(bf16[16,32,16,128]{3,2,1,0:T(8,128)(2,1)} %frames_in.1, bf16[16,32,16,128]{3,2,1,0:T(8,128)(2,1)} %cotangent_in.1, f32[1,128]{1,0:T(1,128)} %bitcast.2, bf16[128,384]{1,0:T(8,128)(2,1)} %w_qkv.1, f32[4,256,256]{2,1,0:T(8,128)} %bias_in.1, ...), custom_call_target="tpu_custom_call" | custom-call | tf_op jit(solution)/shard_map/pallas_call | solution.py:560
  93.9 3.4 %shard_map.129 = (f32[16,32,16,128]{3,2,1,0:T(8,128)}, f32[128,384]{1,0:T(8,128)}, f32[128,128]{1,0:T(8,128)}, f32[128,512]{1,0:T(8,128)}, f32[512,128]{1,0:T(8,128)}) custom-call(bf16[16,32,16,128]{3,2,1,0:T(8,128)(2,1)} %get-tuple-element.7.grad_b, bf16[1536,128]{1,0:T(8,128)(2,1)} %get-tuple-element.8.full_in), custom_call_target="tpu_custom_call" | custom-call | tf_op jit(solution)/shard_map/pallas_call | solution.py:607
